TPU v7x, 128 devices: a whole 4x4x4 slice. The times are simulated.
128 devices in a mesh: dp: 2 (over x_hi), blk: 4 (over z), uly: 16 (over y, x_lo, core).
Axes of the slice: x: 4 (x_hi: 2, x_lo: 2; x = x_hi * 2 + x_lo), y: 4, z: 4, core: 2. Of those that a mesh axis runs over, the one named last changes fastest.
Arguments:
- query_rows: bfloat16 [40960, 4096], P(('dp', 'blk', 'uly')), parts along dimension 0, may hold values from -125 to 125
- key_rows: bfloat16 [40960, 4096], P(('dp', 'blk', 'uly')), parts along dimension 0, may hold values from -125 to 125
- value_rows: bfloat16 [40960, 4096], P(('dp', 'blk', 'uly')), parts along dimension 0, may hold values from -6 to 6
- query_gain: float32 [4096], replicated, may hold values from 0.25 to 1.75
- key_gain: float32 [4096], replicated, may hold values from 0.25 to 1.75
- time_start: int32 [160], replicated, may hold values from -1 to 0
- space_start: int32 [2, 160], replicated, may hold values from -2 to 0
Outputs:
- attended: bfloat16 [40960, 4096], P(('dp', 'blk', 'uly')), parts along dimension 0
There are 2 independent parts, one for each index of `dp`. A program takes and returns all parts, laid end to end along the dimension named above; an argument that names none is the same for every part. Nothing has to cross between parts.
All inputs are finite; a program needn't handle non-finite values.
Results may differ from a plain program's by a relative error of at most 0.0077.
Values may be sent and summed in bfloat16 or wider, within the bound.
A program may use at most 192 MiB of HBM per device.

v0:
```python
import jax
import jax.numpy as jnp
from jax import lax
from jax.sharding import PartitionSpec as P

HD = 128
TILES_H = 4
TILES_W = 5
WIN_T = 2
WIN_H = 3
WIN_W = 3
TILE = 128
NW = 18


EPS = 1e-06
NEGATIVE = -1e30


def padded_2(shard, sides, width):
    for axis, dim in sides:
        size, length = (lax.axis_size(axis), shard.shape[dim])
        up = [(i, (i + 1) % size) for i in range(size - 1)]
        down = [(j, i) for i, j in up]
        last = lax.slice_in_dim(shard, length - width, length, axis=dim)
        initial = lax.slice_in_dim(shard, 0, width, axis=dim)
        before = lax.ppermute(last, axis, up)
        after = lax.ppermute(initial, axis, down)
        shard = jnp.concatenate([before, shard, after], axis=dim)
    return shard


def normalize(rows, gain):
    wide = rows.astype(jnp.float32)
    energy = jnp.mean(wide * wide, axis=-1, keepdims=True)
    return (wide * lax.rsqrt(energy + EPS) * gain).astype(jnp.bfloat16)


def window_coords(tile_ids, starts_time, starts_height, starts_width, grid_time):
    plane = TILES_H * TILES_W
    tile_time = tile_ids // plane
    tile_height = tile_ids % plane // TILES_W
    tile_width = tile_ids % TILES_W
    step_time = jnp.arange(WIN_T, dtype=jnp.int32)
    step_height = jnp.arange(WIN_H, dtype=jnp.int32)
    step_width = jnp.arange(WIN_W, dtype=jnp.int32)
    shape = (tile_ids.shape[0], WIN_T, WIN_H, WIN_W)
    span_time = jnp.broadcast_to(
        (tile_time + starts_time)[:, None, None, None] + step_time[None, :, None, None], shape
    )
    span_height = jnp.broadcast_to(
        (tile_height + starts_height)[:, None, None, None] + step_height[None, None, :, None], shape
    )
    span_width = jnp.broadcast_to(
        (tile_width + starts_width)[:, None, None, None] + step_width[None, None, None, :], shape
    )
    span_time = span_time.reshape(tile_ids.shape[0], -1)
    span_height = span_height.reshape(tile_ids.shape[0], -1)
    span_width = span_width.reshape(tile_ids.shape[0], -1)
    valid = (
        (span_time >= 0) & (span_time < grid_time) & (span_height >= 0) & (span_height < TILES_H)
    )
    valid = valid & (span_width >= 0) & (span_width < TILES_W)
    return (span_time, span_height, span_width, valid)


def attend(queries, keys, values, valid):
    scores = jnp.einsum(
        "bqhd,bkhd->bhqk", queries, keys, preferred_element_type=jnp.float32
    ) * HD ** (-0.5)
    token_valid = jnp.repeat(valid, TILE, axis=1)
    scores = jnp.where(token_valid[:, None, None, :], scores, NEGATIVE)
    top = jnp.max(scores, axis=-1, keepdims=True)
    weights = jnp.exp(scores - top)
    probs = (weights / jnp.sum(weights, axis=-1, keepdims=True)).astype(jnp.bfloat16)
    result = jnp.einsum("bhqk,bkhd->bqhd", probs, values, preferred_element_type=jnp.float32)
    return result.astype(jnp.bfloat16)


def per_device(query_rows, key_rows, value_rows, query_gain, key_gain, time_start, space_start):
    groups = lax.axis_size("uly")
    width = query_rows.shape[1]
    local_width = width // groups
    local_heads = local_width // HD
    sending = (normalize(query_rows, query_gain), normalize(key_rows, key_gain), value_rows)
    query_heads, key_heads, value_heads = (
        lax.all_to_all(sending[0], "uly", split_axis=1, concat_axis=0, tiled=True),
        lax.all_to_all(sending[1], "uly", split_axis=1, concat_axis=0, tiled=True),
        lax.all_to_all(sending[2], "uly", split_axis=1, concat_axis=0, tiled=True),
    )
    slab = query_heads.shape[0]
    plane = TILES_H * TILES_W
    slab_tiles = slab // TILE
    rim = plane * TILE
    paired = jnp.concatenate((key_heads, value_heads), axis=1)
    padded = padded_2(paired, (("blk", 0),), rim)
    ext_tiles = slab_tiles + 2 * plane
    table = padded.reshape(ext_tiles, TILE * 2 * local_width)
    first = lax.axis_index("blk") * slab_tiles
    grid_time = slab_tiles // plane * lax.axis_size("blk")
    local_time = lax.dynamic_slice_in_dim(time_start, first, slab_tiles)
    local_space = lax.dynamic_slice_in_dim(space_start, first, slab_tiles, 1)
    tile_ids = first + jnp.arange(slab_tiles, dtype=jnp.int32)
    span_time, span_height, span_width, valid = window_coords(
        tile_ids, local_time, local_space[0], local_space[1], grid_time
    )
    local_span = span_time - first // plane + 1
    index = jnp.clip((local_span * TILES_H + span_height) * TILES_W + span_width, 0, ext_tiles - 1)
    limit = max(1, 1024 // TILE)
    block_tiles = max(
        (size for size in range(1, min(limit, slab_tiles) + 1) if slab_tiles % size == 0)
    )
    block_count = slab_tiles // block_tiles
    query_blocks = query_heads.reshape(block_count, block_tiles, TILE, local_heads, HD)
    index_blocks = index.reshape(block_count, block_tiles, -1)
    valid_blocks = valid.reshape(block_count, block_tiles, -1)
    columns = jnp.arange(ext_tiles, dtype=jnp.int32)

    def one_block(item):
        queries, block_index, block_valid = item
        selector = (block_index.reshape(-1)[:, None] == columns[None, :]).astype(jnp.bfloat16)
        picked = jnp.dot(selector, table, preferred_element_type=jnp.float32).astype(jnp.bfloat16)
        picked = picked.reshape(block_tiles, NW * TILE, 2, local_heads, HD)
        return attend(queries, picked[:, :, 0], picked[:, :, 1], block_valid)

    attended_heads = lax.map(one_block, (query_blocks, index_blocks, valid_blocks))
    attended_heads = attended_heads.reshape(slab, local_width)
    return lax.all_to_all(attended_heads, "uly", split_axis=0, concat_axis=1, tiled=True)


def solution(mesh):
    placed = (
        P(("dp", "blk", "uly"), None),
        P(("dp", "blk", "uly"), None),
        P(("dp", "blk", "uly"), None),
        P(),
        P(),
        P(),
        P(),
    )
    return jax.shard_map(
        per_device,
        mesh=mesh,
        in_specs=placed,
        out_specs=P(("dp", "blk", "uly"), None),
        check_vma=False,
    )
```

profile of v0, /device:TPU:1, one launch (start us, length us, event | category | flops | bytes accessed | tf_op | source)
XLA Modules:
  0.0 870.2 jit_solution(17070153933962255210)
XLA Ops:
  6.7 6.9 all-to-all-start
  17.2 29.2 %all-to-all-done = bf16[320,16,256]{2,0,1:T(8,128)(2,1)S(1)} async-done(((bf16[320,16,256]{2,0,1:T(8,128)(2,1)}), bf16[320,16,256]{2,0,1:T(8,128)(2,1)S(1)}, u32[]{:S(2)}, u32[]{:S(2)}) %all-to-all-start) | async-done | bytes 2621472 | tf_op jit(solution)/shard_map/all_to_all | solution.py:88
  46.4 5.1 all-to-all-start.1
  53.8 30.6 %all-to-all-done.1 = bf16[320,16,256]{2,0,1:T(8,128)(2,1)} async-done(((bf16[320,16,256]{2,0,1:T(8,128)(2,1)}), bf16[320,16,256]{2,0,1:T(8,128)(2,1)}, u32[]{:S(2)}, u32[]{:S(2)}) %all-to-all-start.1) | async-done | bytes 2621472 | tf_op jit(solution)/shard_map/all_to_all | solution.py:89
  84.4 6.3 fusion.25
  99.7 5.3 all-to-all-start.2
  105.7 32.3 %all-to-all-done.2 = bf16[320,16,256]{2,0,1:T(8,128)(2,1)} async-done(((bf16[320,16,256]{2,0,1:T(8,128)(2,1)}), bf16[320,16,256]{2,0,1:T(8,128)(2,1)}, u32[]{:S(2)}, u32[]{:S(2)}) %all-to-all-start.2) | async-done | bytes 2621472 | tf_op jit(solution)/shard_map/all_to_all | solution.py:87
  142.9 6.9 collective-permute-done
  149.8 5.3 collective-permute-done.1
  155.1 21.5 %pad_maximum_fusion = bf16[10240,512]{1,0:T(8,128)(2,1)} fusion(bf16[2560,512]{1,0:T(8,128)(2,1)} %collective-permute-done.1, bf16[5120,256]{1,0:T(8,128)(2,1)} %bitcast.5, bf16[5120,256]{1,0:T(8,128)(2,1)S(1)} %bitcast.67, bf16[2560,512]{1,0:T(8,128)(2,1)} %collective-permute-done), kind=kLoop, calls=%fused_computation.26 | loop fusion | flops 41943040 | bytes 20971520 | tf_op jit(solution)/shard_map/concatenate | solution.py:29
  176.6 13.0 %reshape.188 = bf16[80,65536]{1,0:T(8,128)(2,1)} reshape(bf16[10240,512]{1,0:T(8,128)(2,1)} %pad_maximum_fusion) | data formatting | bytes 20971520 | tf_op jit(solution)/shard_map/reshape | solution.py:98
  189.7 637.2 %while.11 = (s32[]{:T(128)}, bf16[5,8,128,2,128]{4,3,2,1,0:T(2,128)(2,1)}, s32[5,8,18]{2,1,0:T(8,128)S(1)}, bf16[80,65536]{1,0:T(8,128)(2,1)}, pred[5,8,18]{1,2,...) while((s32[]{:T(128)}, bf16[5,8,128,2,128]{4,3,2,1,0:T(2,128)(2,1)}, ...), condition=%wide.region_5.6_spmd.clone, body=%wide.region_2.5_spmd.clone.sunk | while | flops 3973330432 | bytes 222355280 | solution.py:126
  189.8 13.1 %convolution_convert_fusion.2 = bf16[144,65536]{1,0:T(8,128)(2,1)} fusion(bf16[80,65536]{1,0:T(8,128)(2,1)} %get-tuple-element.168, s32[144]{0:T(256)S(1)} %eq.33), kind=kOutput, calls=%fused_computation.2.clone.1 | convolution fusion | flops 1519398144 | bytes 29360704 | tf_op jit(solution)/shard_map/while/body/eval_jaxpr/dot_general | solution.py:122
  202.9 24.8 %reshape.206 = bf16[8,2304,2,2,128]{4,3,2,1,0:T(2,128)(2,1)} reshape(bf16[144,65536]{1,0:T(8,128)(2,1)} %convolution_convert_fusion.2) | data formatting | bytes 37748736 | tf_op jit(solution)/shard_map/while/body/eval_jaxpr/reshape | solution.py:123
  227.6 16.1 %fusion.43 = (bf16[8,2304,1,2,128]{4,3,2,1,0:T(2,128)(2,1)}, bf16[8,2304,1,2,128]{4,3,2,1,0:T(2,128)(2,1)}) fusion(bf16[8,2304,2,2,128]{4,3,2,1,0:T(2,128)(2,1)} %reshape.206), kind=kLoop, calls=%fused_computation.67.clone.1 | loop fusion | bytes 37748736 | tf_op jit(solution)/shard_map/while/body/eval_jaxpr/slice | solution.py:124
  245.1 12.8 %fusion.44 = f32[8,2,128,2304]{3,2,1,0:T(8,128)} fusion(bf16[8,2304,1,2,128]{4,3,2,1,0:T(2,128)(2,1)} %get-tuple-element.147, bf16[1,8,128,2,128]{4,3,2,1,0:T(2,128)(2,1)S(1)} %constant_dynamic-slice_fusion.6), kind=kOutput, calls=%fused_computation.8.clone.1 | convolution fusion | flops 1207959552 | bytes 28835840 | tf_op jit(solution)/shard_map/while/body/eval_jaxpr/bqhd,bkhd->bhqk/dot_general | solution.py:68
  258.0 22.2 %fusion.45 = (f32[8,2,128]{2,1,0:T(2,128)S(1)}, f32[8,2,128,2304]{3,2,1,0:T(8,128)}) fusion(f32[8,2,128,2304]{3,2,1,0:T(8,128)} %fusion.44, pred[8,2304]{1,0:T(8,128)(4,1)S(1)} %broadcast_bitcast_fusion.2), kind=kOutput, calls=%fused_computation.68.clone.1 | output fusion | flops 28313856 | bytes 37775360 | tf_op jit(solution)/shard_map/while/body/eval_jaxpr/sub | solution.py:74
  280.2 23.5 %copy.74 = bf16[8,2304,1,2,128]{1,4,3,0,2:T(8,128)(2,1)} copy(bf16[8,2304,1,2,128]{4,3,2,1,0:T(2,128)(2,1)} %get-tuple-element.150) | data formatting | bytes 18874368 | tf_op jit(solution)/shard_map/while
  303.7 11.7 %fusion.46 = bf16[1,8,128,2,128]{2,4,3,1,0:T(8,128)(2,1)S(1)} fusion(f32[8,2,128,2304]{3,2,1,0:T(8,128)} %get-tuple-element.148, f32[8,2,128]{2,1,0:T(2,128)S(1)} %get-tuple-element.149, bf16[8,2304,1,2,128]{1,4,3,0,2:T(8,128)(2,1)} %copy.74), kind=kOutput, calls=%fused_computation.15.clone.1 | convolution fusion | flops 1217658880 | bytes 28844032 | tf_op jit(solution)/shard_map/while/body/eval_jaxpr/bhqk,bkhd->bqhd/dot_general | solution.py:76
  317.2 13.1 %convolution_convert_fusion.2 = bf16[144,65536]{1,0:T(8,128)(2,1)} fusion(bf16[80,65536]{1,0:T(8,128)(2,1)} %get-tuple-element.168, s32[144]{0:T(256)S(1)} %eq.33), kind=kOutput, calls=%fused_computation.2.clone.1 | convolution fusion | flops 1519398144 | bytes 29360704 | tf_op jit(solution)/shard_map/while/body/eval_jaxpr/dot_general | solution.py:122
  330.3 24.8 %reshape.206 = bf16[8,2304,2,2,128]{4,3,2,1,0:T(2,128)(2,1)} reshape(bf16[144,65536]{1,0:T(8,128)(2,1)} %convolution_convert_fusion.2) | data formatting | bytes 37748736 | tf_op jit(solution)/shard_map/while/body/eval_jaxpr/reshape | solution.py:123
  355.1 16.1 %fusion.43 = (bf16[8,2304,1,2,128]{4,3,2,1,0:T(2,128)(2,1)}, bf16[8,2304,1,2,128]{4,3,2,1,0:T(2,128)(2,1)}) fusion(bf16[8,2304,2,2,128]{4,3,2,1,0:T(2,128)(2,1)} %reshape.206), kind=kLoop, calls=%fused_computation.67.clone.1 | loop fusion | bytes 37748736 | tf_op jit(solution)/shard_map/while/body/eval_jaxpr/slice | solution.py:124
  372.6 12.8 %fusion.44 = f32[8,2,128,2304]{3,2,1,0:T(8,128)} fusion(bf16[8,2304,1,2,128]{4,3,2,1,0:T(2,128)(2,1)} %get-tuple-element.147, bf16[1,8,128,2,128]{4,3,2,1,0:T(2,128)(2,1)S(1)} %constant_dynamic-slice_fusion.6), kind=kOutput, calls=%fused_computation.8.clone.1 | convolution fusion | flops 1207959552 | bytes 28835840 | tf_op jit(solution)/shard_map/while/body/eval_jaxpr/bqhd,bkhd->bhqk/dot_general | solution.py:68
  385.5 22.2 %fusion.45 = (f32[8,2,128]{2,1,0:T(2,128)S(1)}, f32[8,2,128,2304]{3,2,1,0:T(8,128)}) fusion(f32[8,2,128,2304]{3,2,1,0:T(8,128)} %fusion.44, pred[8,2304]{1,0:T(8,128)(4,1)S(1)} %broadcast_bitcast_fusion.2), kind=kOutput, calls=%fused_computation.68.clone.1 | output fusion | flops 28313856 | bytes 37775360 | tf_op jit(solution)/shard_map/while/body/eval_jaxpr/sub | solution.py:74
  407.7 23.5 %copy.74 = bf16[8,2304,1,2,128]{1,4,3,0,2:T(8,128)(2,1)} copy(bf16[8,2304,1,2,128]{4,3,2,1,0:T(2,128)(2,1)} %get-tuple-element.150) | data formatting | bytes 18874368 | tf_op jit(solution)/shard_map/while
  431.2 11.7 %fusion.46 = bf16[1,8,128,2,128]{2,4,3,1,0:T(8,128)(2,1)S(1)} fusion(f32[8,2,128,2304]{3,2,1,0:T(8,128)} %get-tuple-element.148, f32[8,2,128]{2,1,0:T(2,128)S(1)} %get-tuple-element.149, bf16[8,2304,1,2,128]{1,4,3,0,2:T(8,128)(2,1)} %copy.74), kind=kOutput, calls=%fused_computation.15.clone.1 | convolution fusion | flops 1217658880 | bytes 28844032 | tf_op jit(solution)/shard_map/while/body/eval_jaxpr/bhqk,bkhd->bqhd/dot_general | solution.py:76
  444.6 13.1 %convolution_convert_fusion.2 = bf16[144,65536]{1,0:T(8,128)(2,1)} fusion(bf16[80,65536]{1,0:T(8,128)(2,1)} %get-tuple-element.168, s32[144]{0:T(256)S(1)} %eq.33), kind=kOutput, calls=%fused_computation.2.clone.1 | convolution fusion | flops 1519398144 | bytes 29360704 | tf_op jit(solution)/shard_map/while/body/eval_jaxpr/dot_general | solution.py:122
  457.8 24.8 %reshape.206 = bf16[8,2304,2,2,128]{4,3,2,1,0:T(2,128)(2,1)} reshape(bf16[144,65536]{1,0:T(8,128)(2,1)} %convolution_convert_fusion.2) | data formatting | bytes 37748736 | tf_op jit(solution)/shard_map/while/body/eval_jaxpr/reshape | solution.py:123
  482.5 16.1 %fusion.43 = (bf16[8,2304,1,2,128]{4,3,2,1,0:T(2,128)(2,1)}, bf16[8,2304,1,2,128]{4,3,2,1,0:T(2,128)(2,1)}) fusion(bf16[8,2304,2,2,128]{4,3,2,1,0:T(2,128)(2,1)} %reshape.206), kind=kLoop, calls=%fused_computation.67.clone.1 | loop fusion | bytes 37748736 | tf_op jit(solution)/shard_map/while/body/eval_jaxpr/slice | solution.py:124
  500.0 12.8 %fusion.44 = f32[8,2,128,2304]{3,2,1,0:T(8,128)} fusion(bf16[8,2304,1,2,128]{4,3,2,1,0:T(2,128)(2,1)} %get-tuple-element.147, bf16[1,8,128,2,128]{4,3,2,1,0:T(2,128)(2,1)S(1)} %constant_dynamic-slice_fusion.6), kind=kOutput, calls=%fused_computation.8.clone.1 | convolution fusion | flops 1207959552 | bytes 28835840 | tf_op jit(solution)/shard_map/while/body/eval_jaxpr/bqhd,bkhd->bhqk/dot_general | solution.py:68
  512.9 22.2 %fusion.45 = (f32[8,2,128]{2,1,0:T(2,128)S(1)}, f32[8,2,128,2304]{3,2,1,0:T(8,128)}) fusion(f32[8,2,128,2304]{3,2,1,0:T(8,128)} %fusion.44, pred[8,2304]{1,0:T(8,128)(4,1)S(1)} %broadcast_bitcast_fusion.2), kind=kOutput, calls=%fused_computation.68.clone.1 | output fusion | flops 28313856 | bytes 37775360 | tf_op jit(solution)/shard_map/while/body/eval_jaxpr/sub | solution.py:74
  535.1 23.5 %copy.74 = bf16[8,2304,1,2,128]{1,4,3,0,2:T(8,128)(2,1)} copy(bf16[8,2304,1,2,128]{4,3,2,1,0:T(2,128)(2,1)} %get-tuple-element.150) | data formatting | bytes 18874368 | tf_op jit(solution)/shard_map/while
  558.6 11.7 %fusion.46 = bf16[1,8,128,2,128]{2,4,3,1,0:T(8,128)(2,1)S(1)} fusion(f32[8,2,128,2304]{3,2,1,0:T(8,128)} %get-tuple-element.148, f32[8,2,128]{2,1,0:T(2,128)S(1)} %get-tuple-element.149, bf16[8,2304,1,2,128]{1,4,3,0,2:T(8,128)(2,1)} %copy.74), kind=kOutput, calls=%fused_computation.15.clone.1 | convolution fusion | flops 1217658880 | bytes 28844032 | tf_op jit(solution)/shard_map/while/body/eval_jaxpr/bhqk,bkhd->bqhd/dot_general | solution.py:76
  572.1 13.1 %convolution_convert_fusion.2 = bf16[144,65536]{1,0:T(8,128)(2,1)} fusion(bf16[80,65536]{1,0:T(8,128)(2,1)} %get-tuple-element.168, s32[144]{0:T(256)S(1)} %eq.33), kind=kOutput, calls=%fused_computation.2.clone.1 | convolution fusion | flops 1519398144 | bytes 29360704 | tf_op jit(solution)/shard_map/while/body/eval_jaxpr/dot_general | solution.py:122
  585.2 24.8 %reshape.206 = bf16[8,2304,2,2,128]{4,3,2,1,0:T(2,128)(2,1)} reshape(bf16[144,65536]{1,0:T(8,128)(2,1)} %convolution_convert_fusion.2) | data formatting | bytes 37748736 | tf_op jit(solution)/shard_map/while/body/eval_jaxpr/reshape | solution.py:123
  610.0 16.1 %fusion.43 = (bf16[8,2304,1,2,128]{4,3,2,1,0:T(2,128)(2,1)}, bf16[8,2304,1,2,128]{4,3,2,1,0:T(2,128)(2,1)}) fusion(bf16[8,2304,2,2,128]{4,3,2,1,0:T(2,128)(2,1)} %reshape.206), kind=kLoop, calls=%fused_computation.67.clone.1 | loop fusion | bytes 37748736 | tf_op jit(solution)/shard_map/while/body/eval_jaxpr/slice | solution.py:124
  627.5 12.8 %fusion.44 = f32[8,2,128,2304]{3,2,1,0:T(8,128)} fusion(bf16[8,2304,1,2,128]{4,3,2,1,0:T(2,128)(2,1)} %get-tuple-element.147, bf16[1,8,128,2,128]{4,3,2,1,0:T(2,128)(2,1)S(1)} %constant_dynamic-slice_fusion.6), kind=kOutput, calls=%fused_computation.8.clone.1 | convolution fusion | flops 1207959552 | bytes 28835840 | tf_op jit(solution)/shard_map/while/body/eval_jaxpr/bqhd,bkhd->bhqk/dot_general | solution.py:68
  640.4 22.2 %fusion.45 = (f32[8,2,128]{2,1,0:T(2,128)S(1)}, f32[8,2,128,2304]{3,2,1,0:T(8,128)}) fusion(f32[8,2,128,2304]{3,2,1,0:T(8,128)} %fusion.44, pred[8,2304]{1,0:T(8,128)(4,1)S(1)} %broadcast_bitcast_fusion.2), kind=kOutput, calls=%fused_computation.68.clone.1 | output fusion | flops 28313856 | bytes 37775360 | tf_op jit(solution)/shard_map/while/body/eval_jaxpr/sub | solution.py:74
  662.6 23.5 %copy.74 = bf16[8,2304,1,2,128]{1,4,3,0,2:T(8,128)(2,1)} copy(bf16[8,2304,1,2,128]{4,3,2,1,0:T(2,128)(2,1)} %get-tuple-element.150) | data formatting | bytes 18874368 | tf_op jit(solution)/shard_map/while
  686.1 11.7 %fusion.46 = bf16[1,8,128,2,128]{2,4,3,1,0:T(8,128)(2,1)S(1)} fusion(f32[8,2,128,2304]{3,2,1,0:T(8,128)} %get-tuple-element.148, f32[8,2,128]{2,1,0:T(2,128)S(1)} %get-tuple-element.149, bf16[8,2304,1,2,128]{1,4,3,0,2:T(8,128)(2,1)} %copy.74), kind=kOutput, calls=%fused_computation.15.clone.1 | convolution fusion | flops 1217658880 | bytes 28844032 | tf_op jit(solution)/shard_map/while/body/eval_jaxpr/bhqk,bkhd->bqhd/dot_general | solution.py:76
  699.5 13.1 %convolution_convert_fusion.2 = bf16[144,65536]{1,0:T(8,128)(2,1)} fusion(bf16[80,65536]{1,0:T(8,128)(2,1)} %get-tuple-element.168, s32[144]{0:T(256)S(1)} %eq.33), kind=kOutput, calls=%fused_computation.2.clone.1 | convolution fusion | flops 1519398144 | bytes 29360704 | tf_op jit(solution)/shard_map/while/body/eval_jaxpr/dot_general | solution.py:122
  712.6 24.8 %reshape.206 = bf16[8,2304,2,2,128]{4,3,2,1,0:T(2,128)(2,1)} reshape(bf16[144,65536]{1,0:T(8,128)(2,1)} %convolution_convert_fusion.2) | data formatting | bytes 37748736 | tf_op jit(solution)/shard_map/while/body/eval_jaxpr/reshape | solution.py:123
  737.4 16.1 %fusion.43 = (bf16[8,2304,1,2,128]{4,3,2,1,0:T(2,128)(2,1)}, bf16[8,2304,1,2,128]{4,3,2,1,0:T(2,128)(2,1)}) fusion(bf16[8,2304,2,2,128]{4,3,2,1,0:T(2,128)(2,1)} %reshape.206), kind=kLoop, calls=%fused_computation.67.clone.1 | loop fusion | bytes 37748736 | tf_op jit(solution)/shard_map/while/body/eval_jaxpr/slice | solution.py:124
  754.9 12.8 %fusion.44 = f32[8,2,128,2304]{3,2,1,0:T(8,128)} fusion(bf16[8,2304,1,2,128]{4,3,2,1,0:T(2,128)(2,1)} %get-tuple-element.147, bf16[1,8,128,2,128]{4,3,2,1,0:T(2,128)(2,1)S(1)} %constant_dynamic-slice_fusion.6), kind=kOutput, calls=%fused_computation.8.clone.1 | convolution fusion | flops 1207959552 | bytes 28835840 | tf_op jit(solution)/shard_map/while/body/eval_jaxpr/bqhd,bkhd->bhqk/dot_general | solution.py:68
  767.8 22.2 %fusion.45 = (f32[8,2,128]{2,1,0:T(2,128)S(1)}, f32[8,2,128,2304]{3,2,1,0:T(8,128)}) fusion(f32[8,2,128,2304]{3,2,1,0:T(8,128)} %fusion.44, pred[8,2304]{1,0:T(8,128)(4,1)S(1)} %broadcast_bitcast_fusion.2), kind=kOutput, calls=%fused_computation.68.clone.1 | output fusion | flops 28313856 | bytes 37775360 | tf_op jit(solution)/shard_map/while/body/eval_jaxpr/sub | solution.py:74
  790.0 23.5 %copy.74 = bf16[8,2304,1,2,128]{1,4,3,0,2:T(8,128)(2,1)} copy(bf16[8,2304,1,2,128]{4,3,2,1,0:T(2,128)(2,1)} %get-tuple-element.150) | data formatting | bytes 18874368 | tf_op jit(solution)/shard_map/while
  813.5 11.7 %fusion.46 = bf16[1,8,128,2,128]{2,4,3,1,0:T(8,128)(2,1)S(1)} fusion(f32[8,2,128,2304]{3,2,1,0:T(8,128)} %get-tuple-element.148, f32[8,2,128]{2,1,0:T(2,128)S(1)} %get-tuple-element.149, bf16[8,2304,1,2,128]{1,4,3,0,2:T(8,128)(2,1)} %copy.74), kind=kOutput, calls=%fused_computation.15.clone.1 | convolution fusion | flops 1217658880 | bytes 28844032 | tf_op jit(solution)/shard_map/while/body/eval_jaxpr/bhqk,bkhd->bqhd/dot_general | solution.py:76
  831.1 37.3 %all_to_all.73 = bf16[16,320,256]{2,1,0:T(8,128)(2,1)S(1)} all-to-all(bf16[16,320,256]{2,1,0:T(8,128)(2,1)S(1)} %all_to_all.65), channel_id=1, replica_groups=mesh['dp'=2,'blk'=4,'uly'=16] {'uly'}, dimensions={0} | all-to-all | bytes 5242880 | tf_op jit(solution)/shard_map/all_to_all | solution.py:128
  (74 shorter events, 49.0 us)
Async XLA Ops:
  0.0 105.1 %copy-start = (s32[2,160]{1,0:T(2,128)S(1)}, s32[2,160]{1,0:T(2,128)}, u32[]{:S(2)}) copy-start(s32[2,160]{1,0:T(2,128)} %param.15) | copy-start | bytes 3844
  6.7 39.6 %all-to-all-start = ((bf16[320,16,256]{2,0,1:T(8,128)(2,1)}), bf16[320,16,256]{2,0,1:T(8,128)(2,1)S(1)}, u32[]{:S(2)}, u32[]{:S(2)}) async-start(bf16[320,16,256]{2,0,1:T(8,128)(2,1)} %bitcast.70), calls=%async_computation | async-start | bytes 5242880 | tf_op jit(solution)/shard_map/all_to_all | solution.py:88
  46.4 38.0 %all-to-all-start.1 = ((bf16[320,16,256]{2,0,1:T(8,128)(2,1)}), bf16[320,16,256]{2,0,1:T(8,128)(2,1)}, u32[]{:S(2)}, u32[]{:S(2)}) async-start(bf16[320,16,256]{2,0,1:T(8,128)(2,1)} %bitcast.69), calls=%async_computation.1 | async-start | bytes 5242880 | tf_op jit(solution)/shard_map/all_to_all | solution.py:89
  84.4 12.6 %copy-start.2 = (bf16[320,4096]{1,0:T(8,128)(2,1)S(1)}, bf16[320,4096]{1,0:T(8,128)(2,1)}, u32[]{:S(2)}) copy-start(bf16[320,4096]{1,0:T(8,128)(2,1)} %param.9) | copy-start | bytes 7864324
  84.4 12.6 %copy-start.3 = (f32[4096]{0:T(1024)S(1)}, f32[4096]{0:T(1024)}, u32[]{:S(2)}) copy-start(f32[4096]{0:T(1024)} %param.12) | copy-start | bytes 49156
  90.7 59.1 %collective-permute-start = (bf16[2560,512]{1,0:T(8,128)(2,1)}, bf16[2560,512]{1,0:T(8,128)(2,1)}, u32[]{:S(2)}, u32[]{:S(2)}) collective-permute-start(bf16[2560,512]{1,0:T(8,128)(2,1)} %get-tuple-element.97), channel_id=1, source_target_pairs={{0,16},{16,32},{32,48},{1,17},{17,33},{33,49},{2,18},{18,34},{34,5... | collective-permute-start | bytes 7864328 | tf_op jit(solution)/shard_map/ppermute | solution.py:27
  95.7 59.4 %collective-permute-start.1 = (bf16[2560,512]{1,0:T(8,128)(2,1)}, bf16[2560,512]{1,0:T(8,128)(2,1)}, u32[]{:S(2)}, u32[]{:S(2)}) collective-permute-start(bf16[2560,512]{1,0:T(8,128)(2,1)} %get-tuple-element.98), channel_id=1, source_target_pairs={{16,0},{32,16},{48,32},{17,1},{33,17},{49,33},{18,2},{34,18},{50,3... | collective-permute-start | bytes 7864328 | tf_op jit(solution)/shard_map/ppermute | solution.py:28
  97.9 7.3 copy-start.4
  99.7 38.3 %all-to-all-start.2 = ((bf16[320,16,256]{2,0,1:T(8,128)(2,1)}), bf16[320,16,256]{2,0,1:T(8,128)(2,1)}, u32[]{:S(2)}, u32[]{:S(2)}) async-start(bf16[320,16,256]{2,0,1:T(8,128)(2,1)} %bitcast.68), calls=%async_computation.2 | async-start | bytes 5242880 | tf_op jit(solution)/shard_map/all_to_all | solution.py:87
  826.9 43.3 %copy-start.1 = (s32[2,160]{1,0:T(2,128)S(1)}, s32[2,160]{1,0:T(2,128)}, u32[]{:S(2)}) copy-start(s32[2,160]{1,0:T(2,128)} %param.15) | copy-start | bytes 3844
where the time goes:
time: 877 us; the launch traced here: 870 us
  local copies, waits for them, and re-layouts  369 us (42%)
  matrix products  188 us (21%)
  other arithmetic  147 us (17%)
  waiting for transfers between devices  104 us (12%)
  blocking collectives  37.3 us (4%)
  starting transfers between devices  23.6 us (3%)
    reshape x5, local copies, waits for them, and re-layouts, one_block(): picked = picked.reshape(block_tiles, NW * TILE, 2, local_heads, HD)  124 us
    while x5, local copies, waits for them, and re-layouts  117 us
    sub x5, other arithmetic, attend(): weights = jnp.exp(scores - top)  111 us
    slice x5, local copies, waits for them, and re-layouts, one_block(): return attend(queries, picked[:, :, 0], picked[:, :, 1], block_valid)  80.4 us
    dot_general x5, matrix products, one_block(): jnp.dot(selector, table, preferred_element_type=jnp.float32)  65.6 us
    dot_general x5, matrix products, attend(): jnp.einsum('bqhd,bkhd->bhqk', queries, keys, preferred_element_type=jnp.f...  64 us
    dot_general x5, matrix products, attend(): jnp.einsum('bhqk,bkhd->bqhd', probs, values, preferred_element_type=jnp.f...  58.7 us
    all_to_all x1, blocking collectives, per_device(): lax.all_to_all(attended_heads, 'uly', split_axis=0, concat_axis=1, tiled=...  37.3 us
  transfers between devices with their start and end apart: 5, of which 5 were waited for; matrix products, arithmetic and copies ran while one was open for 2% of the time, Pallas kernels for 0%

commit v1 on v0

v1 whole, which is shorter than its diff:
```python
import math

import jax
import jax.numpy as jnp
from jax import lax
from jax.experimental import pallas as pl
from jax.experimental.pallas import tpu as pltpu
from jax.sharding import PartitionSpec as P

HD = 128
TILES_H = 4
TILES_W = 5
WIN_T = 2
WIN_H = 3
WIN_W = 3
TILE = 128
NW = 18
PLANE = TILES_H * TILES_W

EPS = 1e-06
TO_EXP2 = HD ** (-0.5) * math.log2(math.e)
ONES = 16
GROUP_QK = 6
GROUP_PV = 9


def normalize(rows, gain):
    wide = rows.astype(jnp.float32)
    energy = jnp.mean(wide * wide, axis=-1, keepdims=True)
    return (wide * lax.rsqrt(energy + EPS) * gain).astype(jnp.bfloat16)


def window_tables(time_start, space_start, slab_tiles):
    first = lax.axis_index("blk") * slab_tiles
    grid_time = slab_tiles // PLANE * lax.axis_size("blk")
    starts_time = lax.dynamic_slice_in_dim(time_start, first, slab_tiles)
    starts_space = lax.dynamic_slice_in_dim(space_start, first, slab_tiles, 1)
    local = jnp.arange(slab_tiles, dtype=jnp.int32)
    tile_ids = first + local
    slot = jnp.arange(NW, dtype=jnp.int32)[None, :]
    span_time = (tile_ids // PLANE + starts_time)[:, None] + slot // (WIN_H * WIN_W)
    span_height = (tile_ids % PLANE // TILES_W + starts_space[0])[:, None] + slot // WIN_W % WIN_H
    span_width = (tile_ids % TILES_W + starts_space[1])[:, None] + slot % WIN_W
    valid = (span_time >= 0) & (span_time < grid_time)
    valid = valid & (span_height >= 0) & (span_height < TILES_H)
    valid = valid & (span_width >= 0) & (span_width < TILES_W)
    local_time = span_time - first // PLANE + 1
    index = (local_time * TILES_H + span_height) * TILES_W + span_width
    own = (local + PLANE)[:, None]
    zero_tile = slab_tiles + 2 * PLANE
    key_tile = jnp.where(valid, index, own)
    value_tile = jnp.where(valid, index, zero_tile)
    return key_tile.reshape(-1).astype(jnp.int32), value_tile.reshape(-1).astype(jnp.int32)


def tile_rows(tile):
    return pl.ds(pl.multiple_of(tile * TILE, TILE), TILE)


def score_pair(key_tile, tile_a, tile_b, keys, query_a, query_b, scores):
    zero = jnp.zeros((TILE, HD), jnp.bfloat16)
    diagonal = jnp.concatenate(
        [
            jnp.concatenate([query_a.T, zero], axis=1),
            jnp.concatenate([zero, query_b.T], axis=1),
        ],
        axis=0,
    )
    top = None
    for begin in range(0, NW, GROUP_QK):
        parts = []
        for slot in range(begin, begin + GROUP_QK):
            part_a = keys[tile_rows(key_tile[tile_a * NW + slot]), :]
            part_b = keys[tile_rows(key_tile[tile_b * NW + slot]), :]
            parts.append(jnp.concatenate([part_a, part_b], axis=1))
        block = jnp.dot(
            jnp.concatenate(parts, axis=0), diagonal, preferred_element_type=jnp.float32
        )
        scores[begin * TILE : (begin + GROUP_QK) * TILE, :] = block
        partial = jnp.max(block.reshape(GROUP_QK * TILE // 8, 8, 2 * TILE), axis=0)
        top = partial if top is None else jnp.maximum(top, partial)
    return jnp.max(top, axis=0, keepdims=True)


def weigh_pair(value_tile, tile_a, tile_b, values_t, scores, top):
    shift = top * TO_EXP2
    total = None
    for begin in range(0, NW, GROUP_PV):
        weights = jnp.exp2(
            scores[begin * TILE : (begin + GROUP_PV) * TILE, :] * TO_EXP2 - shift
        ).astype(jnp.bfloat16)
        picked = [
            jnp.concatenate(
                [values_t[value_tile[tile * NW + begin + i]] for i in range(GROUP_PV)], axis=1
            )
            for tile in (tile_a, tile_b)
        ]
        part = jnp.dot(
            jnp.concatenate(picked, axis=0), weights, preferred_element_type=jnp.float32
        )
        total = part if total is None else total + part
    high = HD + ONES
    out_a = total[:HD, :TILE] * (1.0 / total[HD : HD + 1, :TILE])
    out_b = total[high : high + HD, TILE:] * (1.0 / total[high + HD : high + HD + 1, TILE:])
    return out_a.T.astype(jnp.bfloat16), out_b.T.astype(jnp.bfloat16)


def attend_head(key_tile, value_tile, queries, keys, values_t, store, scores_a, scores_b, tiles):
    def query(tile):
        return queries[tile_rows(tile), :]

    def step(i, top_a):
        tile = 4 * i
        top_b = score_pair(
            key_tile, tile + 2, tile + 3, keys, query(tile + 2), query(tile + 3), scores_b
        )
        out = weigh_pair(value_tile, tile, tile + 1, values_t, scores_a, top_a)
        store(tile, out[0])
        store(tile + 1, out[1])
        later = jnp.minimum(tile + 4, tiles - 4)
        top_a = score_pair(
            key_tile, later, later + 1, keys, query(later), query(later + 1), scores_a
        )
        out = weigh_pair(value_tile, tile + 2, tile + 3, values_t, scores_b, top_b)
        store(tile + 2, out[0])
        store(tile + 3, out[1])
        return top_a

    top = score_pair(key_tile, 0, 1, keys, query(0), query(1), scores_a)
    lax.fori_loop(0, tiles // 4, step, top)


def attention_kernel(
    key_tile, value_tile, q_hbm, k_hbm, v_hbm, k_low, k_high, v_low, v_high, out,
    queries, keys, values, values_t, scores_a, scores_b, sems,
):
    slab = q_hbm.shape[0]
    tiles = slab // TILE
    rim = PLANE * TILE
    heads = queries.shape[0]
    copies = []
    for head in range(heads):
        columns = pl.ds(head * HD, HD)
        pairs = [
            (v_low, values.at[head, pl.ds(0, rim)]),
            (v_hbm, values.at[head, pl.ds(rim, slab)]),
            (v_high, values.at[head, pl.ds(rim + slab, rim)]),
            (k_low, keys.at[head, pl.ds(0, rim)]),
            (k_hbm, keys.at[head, pl.ds(rim, slab)]),
            (k_high, keys.at[head, pl.ds(rim + slab, rim)]),
            (q_hbm, queries.at[head]),
        ]
        for source, target in pairs:
            copies.append(
                pltpu.make_async_copy(source.at[:, columns], target, sems.at[len(copies)])
            )
    for copy in copies:
        copy.start()
    ones = jnp.ones((ONES, TILE), jnp.bfloat16)
    per_head = len(copies) // heads
    for head in range(heads):
        for copy in copies[head * per_head : (head + 1) * per_head]:
            copy.wait()

        def turn(tile, carry):
            values_t[head, tile, :HD, :] = values[head, tile_rows(tile), :].T
            values_t[head, tile, HD:, :] = ones
            return carry

        lax.fori_loop(0, tiles + 2 * PLANE, turn, 0, unroll=8)
        values_t[head, tiles + 2 * PLANE] = jnp.zeros((HD + ONES, TILE), jnp.bfloat16)

        def store(tile, block):
            out[tile_rows(tile), head * HD : (head + 1) * HD] = block

        attend_head(
            key_tile, value_tile, queries.at[head], keys.at[head], values_t.at[head],
            store, scores_a, scores_b, tiles,
        )


def attention(key_tile, value_tile, query, key, value, key_low, key_high, value_low, value_high):
    slab, width = query.shape
    heads = width // HD
    extended = slab + 2 * PLANE * TILE
    anywhere = pl.BlockSpec(memory_space=pl.ANY)
    return pl.pallas_call(
        attention_kernel,
        out_shape=jax.ShapeDtypeStruct((slab, width), jnp.bfloat16),
        in_specs=[pl.BlockSpec(memory_space=pltpu.SMEM)] * 2 + [anywhere] * 7,
        out_specs=pl.BlockSpec(memory_space=pltpu.VMEM),
        scratch_shapes=[
            pltpu.VMEM((heads, slab, HD), jnp.bfloat16),
            pltpu.VMEM((heads, extended, HD), jnp.bfloat16),
            pltpu.VMEM((heads, extended, HD), jnp.bfloat16),
            pltpu.VMEM((heads, extended // TILE + 1, HD + ONES, TILE), jnp.bfloat16),
            pltpu.VMEM((NW * TILE, 2 * TILE), jnp.float32),
            pltpu.VMEM((NW * TILE, 2 * TILE), jnp.float32),
            pltpu.SemaphoreType.DMA((7 * heads,)),
        ],
        compiler_params=pltpu.CompilerParams(vmem_limit_bytes=48 * 2**20),
        cost_estimate=pl.CostEstimate(
            flops=4 * slab * NW * TILE * width,
            bytes_accessed=10 * slab * width,
            transcendentals=slab * NW * TILE * heads,
        ),
    )(key_tile, value_tile, query, key, value, key_low, key_high, value_low, value_high)


def halo(rows):
    size = lax.axis_size("blk")
    rim = PLANE * TILE
    up = [(i, i + 1) for i in range(size - 1)]
    down = [(i + 1, i) for i in range(size - 1)]
    below = lax.ppermute(rows[rows.shape[0] - rim :], "blk", up)
    above = lax.ppermute(rows[:rim], "blk", down)
    return below, above


def per_device(query_rows, key_rows, value_rows, query_gain, key_gain, time_start, space_start):
    def to_heads(rows):
        return lax.all_to_all(rows, "uly", split_axis=1, concat_axis=0, tiled=True)

    value = to_heads(value_rows)
    key = to_heads(normalize(key_rows, key_gain))
    query = to_heads(normalize(query_rows, query_gain))
    value_low, value_high = halo(value)
    key_low, key_high = halo(key)
    key_tile, value_tile = window_tables(time_start, space_start, query.shape[0] // TILE)
    attended = attention(
        key_tile, value_tile, query, key, value, key_low, key_high, value_low, value_high
    )
    return lax.all_to_all(attended, "uly", split_axis=0, concat_axis=1, tiled=True)


def solution(mesh):
    rows = P(("dp", "blk", "uly"), None)
    return jax.shard_map(
        per_device,
        mesh=mesh,
        in_specs=(rows, rows, rows, P(), P(), P(), P()),
        out_specs=rows,
        check_vma=False,
    )
```

time: 877 us -> 246 us (0.28)
  local copies, waits for them, and re-layouts: 369 us -> 16.1 us
  matrix products: 188 us -> 0 us
  other arithmetic: 147 us -> 5.75 us
  Pallas kernels: 0 us -> 46.8 us
    dot_general x15 -> x0, matrix products: 188 us -> none  [the longest x5 65.6 us: one_block(): jnp.dot(selector, table, preferred_element_type=jnp.float32)]
    reshape x7 -> x0, local copies, waits for them, and re-layouts: 142 us -> none  [the longest x5 124 us: one_block(): picked = picked.reshape(block_tiles, NW * TILE, 2, local_heads, HD)]
    while x5 -> x0, local copies, waits for them, and re-layouts: 117 us -> none
    sub x5 -> x0, other arithmetic: 111 us -> none  [attend(): weights = jnp.exp(scores - top)]
    slice x5 -> x2, local copies, waits for them, and re-layouts: 80.4 us -> 5.31 us  [halo(): above = lax.ppermute(rows[:rim], 'blk', down)]
    pallas_call x0 -> x1, Pallas kernels: none -> 46.8 us  [attention(): pl.pallas_call(attention_kernel, out_shape=jax.ShapeDtypeStruct((slab, wi...]
    concatenate x2 -> x0, other arithmetic: 27.8 us -> none  [the longest x1 21.5 us: padded_2(): shard = jnp.concatenate([before, shard, after], axis=dim)]
    ppermute x2 -> x4, waiting for transfers between devices: 12.2 us -> 34.6 us  [the longest x2 26.5 us: halo(): below = lax.ppermute(rows[rows.shape[0] - rim:], 'blk', up)]
  transfers between devices with their start and end apart: 5 -> 7, of which waited for: 5 -> 7; matrix products, arithmetic and copies ran while one was open for 2% -> 5% of each run, Pallas kernels for 0% -> 0%
where the time goes in v1:
time: 246 us
  waiting for transfers between devices  109 us (44%)
  Pallas kernels  46.8 us (19%)
  blocking collectives  39 us (16%)
  starting transfers between devices  28.8 us (12%)
  local copies, waits for them, and re-layouts  16.1 us (7%)
  other arithmetic  5.75 us (2%)
    all_to_all x3, waiting for transfers between devices, to_heads(): return lax.all_to_all(rows, 'uly', split_axis=1, concat_axis=0, tiled=True)  74.4 us
    pallas_call x1, Pallas kernels, attention(): pl.pallas_call(attention_kernel, out_shape=jax.ShapeDtypeStruct((slab, wi...  46.8 us
    all_to_all x1, blocking collectives, per_device(): lax.all_to_all(attended, 'uly', split_axis=0, concat_axis=1, tiled=True)  39 us
    ppermute x2, waiting for transfers between devices, halo(): below = lax.ppermute(rows[rows.shape[0] - rim:], 'blk', up)  26.5 us
    all_to_all x3, starting transfers between devices, to_heads(): return lax.all_to_all(rows, 'uly', split_axis=1, concat_axis=0, tiled=True)  17.3 us
    ppermute x2, starting transfers between devices, halo(): below = lax.ppermute(rows[rows.shape[0] - rim:], 'blk', up)  8.85 us
    ppermute x2, waiting for transfers between devices, halo(): above = lax.ppermute(rows[:rim], 'blk', down)  8.1 us
    all_to_all x3, local copies, waits for them, and re-layouts, to_heads(): return lax.all_to_all(rows, 'uly', split_axis=1, concat_axis=0, tiled=True)  6.98 us
  transfers between devices with their start and end apart: 7, of which 7 were waited for; matrix products, arithmetic and copies ran while one was open for 5% of the time, Pallas kernels for 0%

profile of v1, /device:TPU:1, one launch (start us, length us, event | category | flops | bytes accessed | tf_op | source)
XLA Modules:
  0.0 245.5 jit_solution(16857024479051609965)
XLA Ops:
  0.0 0.0 copy-start
  0.0 0.0 copy-start.1
  0.0 2.5 %fusion.3 = f32[320]{0:T(512)S(1)} fusion(bf16[320,4096]{1,0:T(8,128)(2,1)} %param.8), kind=kLoop, calls=%fused_computation.7 | loop fusion | flops 3931840 | bytes 2622720 | tf_op jit(solution)/shard_map/reduce_sum | solution.py:29
  2.5 0.0 copy-done.1
  2.5 1.6 fusion.5
  4.1 1.8 copy.24
  5.9 6.9 %all-to-all-start.1 = ((bf16[320,16,256]{2,0,1:T(8,128)(2,1)}), bf16[320,16,256]{2,0,1:T(8,128)(2,1)S(1)}, u32[]{:S(2)}, u32[]{:S(2)}) async-start(bf16[320,16,256]{2,0,1:T(8,128)(2,1)} %bitcast.36), calls=%async_computation.1 | async-start | bytes 5242880 | tf_op jit(solution)/shard_map/all_to_all | solution.py:222
  12.8 3.5 %copy.23 = bf16[40,16,8,256]{3,2,0,1:T(8,128)(2,1)} copy(bf16[40,16,8,256]{3,2,1,0:T(8,128)(2,1)} %bitcast.40) | data formatting | bytes 5242880 | tf_op jit(solution)/shard_map/all_to_all | solution.py:222
  16.3 29.3 %all-to-all-done.1 = bf16[320,16,256]{2,0,1:T(8,128)(2,1)S(1)} async-done(((bf16[320,16,256]{2,0,1:T(8,128)(2,1)}), bf16[320,16,256]{2,0,1:T(8,128)(2,1)S(1)}, u32[]{:S(2)}, u32[]{:S(2)}) %all-to-all-start.1) | async-done | bytes 2621472 | tf_op jit(solution)/shard_map/all_to_all | solution.py:222
  45.5 0.0 copy-start.3
  45.5 1.5 copy-done.3
  47.0 0.0 copy-start.2
  47.0 5.3 %all-to-all-start.2 = ((bf16[320,16,256]{2,0,1:T(8,128)(2,1)}), bf16[320,16,256]{2,0,1:T(8,128)(2,1)}, u32[]{:S(2)}, u32[]{:S(2)}) async-start(bf16[320,16,256]{2,0,1:T(8,128)(2,1)} %bitcast.35), calls=%async_computation.2 | async-start | bytes 5242880 | tf_op jit(solution)/shard_map/all_to_all | solution.py:222
  52.4 0.0 copy-done.2
  52.4 0.0 copy-start.5
  52.4 0.6 fusion
  53.0 0.1 copy-done.5
  53.1 0.9 fusion.2
  54.0 1.8 copy.25
  55.7 29.6 %all-to-all-done.2 = bf16[320,16,256]{2,0,1:T(8,128)(2,1)} async-done(((bf16[320,16,256]{2,0,1:T(8,128)(2,1)}), bf16[320,16,256]{2,0,1:T(8,128)(2,1)}, u32[]{:S(2)}, u32[]{:S(2)}) %all-to-all-start.2) | async-done | bytes 2621472 | tf_op jit(solution)/shard_map/all_to_all | solution.py:222
  85.3 5.1 %all-to-all-start = ((bf16[320,16,256]{2,0,1:T(8,128)(2,1)}), bf16[320,16,256]{2,0,1:T(8,128)(2,1)}, u32[]{:S(2)}, u32[]{:S(2)}) async-start(bf16[320,16,256]{2,0,1:T(8,128)(2,1)} %bitcast.32), calls=%async_computation | async-start | bytes 5242880 | tf_op jit(solution)/shard_map/all_to_all | solution.py:222
  90.4 0.0 copy-start.4
  90.4 3.6 %fusion.19 = (bf16[8,320,256]{2,1,0:T(8,128)(2,1)}, bf16[8,320,256]{2,1,0:T(8,128)(2,1)}) fusion(bf16[16,320,256]{2,1,0:T(8,128)(2,1)} %bitcast.6), kind=kLoop, calls=%fused_computation.55 | loop fusion | bytes 5242880 | tf_op jit(solution)/shard_map/slice | solution.py:216
  94.0 3.6 %collective-permute-start.2 = (bf16[2560,256]{1,0:T(8,128)(2,1)}, bf16[2560,256]{1,0:T(8,128)(2,1)S(1)}, u32[]{:S(2)}, u32[]{:S(2)}) collective-permute-start(bf16[2560,256]{1,0:T(8,128)(2,1)} %bitcast.10), channel_id=1, source_target_pairs={{0,16},{16,32},{32,48},{1,17},{17,33},{33,49},{2,18},{18,34},{34,5... | collective-permute-start | bytes 3932168 | tf_op jit(solution)/shard_map/ppermute | solution.py:215
  97.6 1.3 collective-permute-start.3
  98.9 0.0 copy-done.4
  98.9 0.0 copy-start.6
  98.9 1.8 fusion.20
  100.7 5.2 %collective-permute-start = (bf16[2560,256]{1,0:T(8,128)(2,1)}, bf16[2560,256]{1,0:T(8,128)(2,1)}, u32[]{:S(2)}, u32[]{:S(2)}) collective-permute-start(bf16[2560,256]{1,0:T(8,128)(2,1)} %bitcast.8), channel_id=1, source_target_pairs={{0,16},{16,32},{32,48},{1,17},{17,33},{33,49},{2,18},{18,34},{34,5... | collective-permute-start | bytes 3932168 | tf_op jit(solution)/shard_map/ppermute | solution.py:215
  105.9 1.3 collective-permute-start.1
  107.2 0.0 copy-done
  107.3 0.1 constant_dynamic-slice_fusion
  107.3 0.0 copy-done.6
  107.3 0.1 bitcast_add_fusion
  107.4 0.1 fusion.15
  107.5 0.1 reshape.187.value_tile
  107.6 0.1 reshape.185.key_tile
  107.7 15.6 %all-to-all-done = bf16[320,16,256]{2,0,1:T(8,128)(2,1)} async-done(((bf16[320,16,256]{2,0,1:T(8,128)(2,1)}), bf16[320,16,256]{2,0,1:T(8,128)(2,1)}, u32[]{:S(2)}, u32[]{:S(2)}) %all-to-all-start) | async-done | bytes 2621472 | tf_op jit(solution)/shard_map/all_to_all | solution.py:222
  123.3 2.4 collective-permute-done.2.v_low
  125.7 4.0 %collective-permute-done.3.v_high = bf16[2560,256]{1,0:T(8,128)(2,1)S(1)} collective-permute-done((bf16[2560,256]{1,0:T(8,128)(2,1)}, bf16[2560,256]{1,0:T(8,128)(2,1)S(1)}, u32[]{:S(2)}, u32[]{:S(2)}) %collective-permute-start.3) | collective-permute-done | bytes 1310752 | tf_op jit(solution)/shard_map/ppermute | solution.py:216
  129.7 24.1 %collective-permute-done.k_low = bf16[2560,256]{1,0:T(8,128)(2,1)} collective-permute-done((bf16[2560,256]{1,0:T(8,128)(2,1)}, bf16[2560,256]{1,0:T(8,128)(2,1)}, u32[]{:S(2)}, u32[]{:S(2)}) %collective-permute-start) | collective-permute-done | bytes 1310752 | tf_op jit(solution)/shard_map/ppermute | solution.py:215
  153.8 4.1 %collective-permute-done.1.k_high = bf16[2560,256]{1,0:T(8,128)(2,1)} collective-permute-done((bf16[2560,256]{1,0:T(8,128)(2,1)}, bf16[2560,256]{1,0:T(8,128)(2,1)}, u32[]{:S(2)}, u32[]{:S(2)}) %collective-permute-start.1) | collective-permute-done | bytes 1310752 | tf_op jit(solution)/shard_map/ppermute | solution.py:216
  157.9 46.8 %shard_map.73 = bf16[5120,256]{1,0:T(8,128)(2,1)} custom-call(s32[720]{0:T(1024)S(1)} %reshape.185.key_tile, s32[720]{0:T(1024)S(1)} %reshape.187.value_tile, bf16[5120,256]{1,0:T(8,128)(2,1)} %bitcast.3.q_hbm, bf16[5120,256]{1,0:T(8,128)(2,1)} %bitcast.33, bf16[5120,256]{1,0:T(8,128)(2,1)} %bitcast.7.v_hbm, bf16[2560,256]{1,0:T(8,128)(2,1)} %collective-permute-done.k_low, ...), custom_call_target="tpu_custom_call" | custom-call | flops 12079595520 | bytes 13107200 | tf_op jit(solution)/shard_map/pallas_call | solution.py:187
  204.7 39.0 %all_to_all.76 = bf16[16,320,256]{2,1,0:T(8,128)(2,1)S(1)} all-to-all(bf16[16,320,256]{2,1,0:T(8,128)(2,1)} %bitcast.41), channel_id=1, replica_groups=mesh['dp'=2,'blk'=4,'uly'=16] {'uly'}, dimensions={0} | all-to-all | bytes 5242880 | tf_op jit(solution)/shard_map/all_to_all | solution.py:233
  243.7 1.8 copy.19
  (5 shorter events, 0.1 us)
Async XLA Ops:
  0.0 107.2 %copy-start = (s32[2,160]{1,0:T(2,128)S(1)}, s32[2,160]{1,0:T(2,128)}, u32[]{:S(2)}) copy-start(s32[2,160]{1,0:T(2,128)} %param.13) | copy-start | bytes 3844
  0.0 2.5 %copy-start.1 = (bf16[320,4096]{1,0:T(8,128)(2,1)S(1)}, bf16[320,4096]{1,0:T(8,128)(2,1)}, u32[]{:S(2)}) copy-start(bf16[320,4096]{1,0:T(8,128)(2,1)} %param.8) | copy-start | bytes 7864324
  5.9 39.6 %all-to-all-start.1 = ((bf16[320,16,256]{2,0,1:T(8,128)(2,1)}), bf16[320,16,256]{2,0,1:T(8,128)(2,1)S(1)}, u32[]{:S(2)}, u32[]{:S(2)}) async-start(bf16[320,16,256]{2,0,1:T(8,128)(2,1)} %bitcast.36), calls=%async_computation.1 | async-start | bytes 5242880 | tf_op jit(solution)/shard_map/all_to_all | solution.py:222
  45.5 1.5 copy-start.3
  47.0 5.3 %copy-start.2 = (bf16[320,4096]{1,0:T(8,128)(2,1)S(1)}, bf16[320,4096]{1,0:T(8,128)(2,1)}, u32[]{:S(2)}) copy-start(bf16[320,4096]{1,0:T(8,128)(2,1)} %param.7) | copy-start | bytes 7864324
  47.0 38.3 %all-to-all-start.2 = ((bf16[320,16,256]{2,0,1:T(8,128)(2,1)}), bf16[320,16,256]{2,0,1:T(8,128)(2,1)}, u32[]{:S(2)}, u32[]{:S(2)}) async-start(bf16[320,16,256]{2,0,1:T(8,128)(2,1)} %bitcast.35), calls=%async_computation.2 | async-start | bytes 5242880 | tf_op jit(solution)/shard_map/all_to_all | solution.py:222
  52.4 0.7 copy-start.5
  85.3 38.0 %all-to-all-start = ((bf16[320,16,256]{2,0,1:T(8,128)(2,1)}), bf16[320,16,256]{2,0,1:T(8,128)(2,1)}, u32[]{:S(2)}, u32[]{:S(2)}) async-start(bf16[320,16,256]{2,0,1:T(8,128)(2,1)} %bitcast.32), calls=%async_computation | async-start | bytes 5242880 | tf_op jit(solution)/shard_map/all_to_all | solution.py:222
  90.4 8.5 %copy-start.4 = (bf16[320,16,256]{2,0,1:T(8,128)(2,1)S(1)}, bf16[320,16,256]{2,0,1:T(8,128)(2,1)}, u32[]{:S(2)}) copy-start(bf16[320,16,256]{2,0,1:T(8,128)(2,1)} %copy-done.3) | copy-start | bytes 7864324
  94.0 31.7 %collective-permute-start.2 = (bf16[2560,256]{1,0:T(8,128)(2,1)}, bf16[2560,256]{1,0:T(8,128)(2,1)S(1)}, u32[]{:S(2)}, u32[]{:S(2)}) collective-permute-start(bf16[2560,256]{1,0:T(8,128)(2,1)} %bitcast.10), channel_id=1, source_target_pairs={{0,16},{16,32},{32,48},{1,17},{17,33},{33,49},{2,18},{18,34},{34,5... | collective-permute-start | bytes 3932168 | tf_op jit(solution)/shard_map/ppermute | solution.py:215
  97.6 32.1 %collective-permute-start.3 = (bf16[2560,256]{1,0:T(8,128)(2,1)}, bf16[2560,256]{1,0:T(8,128)(2,1)S(1)}, u32[]{:S(2)}, u32[]{:S(2)}) collective-permute-start(bf16[2560,256]{1,0:T(8,128)(2,1)} %bitcast.11), channel_id=1, source_target_pairs={{16,0},{32,16},{48,32},{17,1},{33,17},{49,33},{18,2},{34,18},{50,3... | collective-permute-start | bytes 3932168 | tf_op jit(solution)/shard_map/ppermute | solution.py:216
  98.9 8.5 %copy-start.6 = (s32[160]{0:T(256)S(1)}, s32[160]{0:T(256)}, u32[]{:S(2)}) copy-start(s32[160]{0:T(256)} %param.12) | copy-start | bytes 1924
  100.7 53.1 %collective-permute-start = (bf16[2560,256]{1,0:T(8,128)(2,1)}, bf16[2560,256]{1,0:T(8,128)(2,1)}, u32[]{:S(2)}, u32[]{:S(2)}) collective-permute-start(bf16[2560,256]{1,0:T(8,128)(2,1)} %bitcast.8), channel_id=1, source_target_pairs={{0,16},{16,32},{32,48},{1,17},{17,33},{33,49},{2,18},{18,34},{34,5... | collective-permute-start | bytes 3932168 | tf_op jit(solution)/shard_map/ppermute | solution.py:215
  105.9 52.0 %collective-permute-start.1 = (bf16[2560,256]{1,0:T(8,128)(2,1)}, bf16[2560,256]{1,0:T(8,128)(2,1)}, u32[]{:S(2)}, u32[]{:S(2)}) collective-permute-start(bf16[2560,256]{1,0:T(8,128)(2,1)} %bitcast.9), channel_id=1, source_target_pairs={{16,0},{32,16},{48,32},{17,1},{33,17},{49,33},{18,2},{34,18},{50,3... | collective-permute-start | bytes 3932168 | tf_op jit(solution)/shard_map/ppermute | solution.py:216

commit v2 on v1

v2 whole, which is shorter than its diff:
```python
import math

import jax
import jax.numpy as jnp
from jax import lax
from jax.experimental import pallas as pl
from jax.experimental.pallas import tpu as pltpu
from jax.sharding import PartitionSpec as P

HD = 128
TILES_H = 4
TILES_W = 5
WIN_T = 2
WIN_H = 3
WIN_W = 3
TILE = 128
HALF = TILE // 2
NW = 18
PLANE = TILES_H * TILES_W
MESH = pl.DeviceIdType.MESH

EPS = 1e-06
TO_EXP2 = HD ** (-0.5) * math.log2(math.e)
ONES = 16
GROUP_QK = 6
GROUP_PV = 9


def window_tables(time_start, space_start, slab_tiles):
    first = lax.axis_index("blk") * slab_tiles
    grid_time = slab_tiles // PLANE * lax.axis_size("blk")
    starts_time = lax.dynamic_slice_in_dim(time_start, first, slab_tiles)
    starts_space = lax.dynamic_slice_in_dim(space_start, first, slab_tiles, 1)
    local = jnp.arange(slab_tiles, dtype=jnp.int32)
    tile_ids = first + local
    slot = jnp.arange(NW, dtype=jnp.int32)[None, :]
    span_time = (tile_ids // PLANE + starts_time)[:, None] + slot // (WIN_H * WIN_W)
    span_height = (tile_ids % PLANE // TILES_W + starts_space[0])[:, None] + slot // WIN_W % WIN_H
    span_width = (tile_ids % TILES_W + starts_space[1])[:, None] + slot % WIN_W
    valid = (span_time >= 0) & (span_time < grid_time)
    valid = valid & (span_height >= 0) & (span_height < TILES_H)
    valid = valid & (span_width >= 0) & (span_width < TILES_W)
    local_time = span_time - first // PLANE + 1
    index = (local_time * TILES_H + span_height) * TILES_W + span_width
    own = (local + PLANE)[:, None]
    zero_tile = slab_tiles + 2 * PLANE
    key_tile = jnp.where(valid, index, own)
    value_tile = jnp.where(valid, index, zero_tile)
    return key_tile.reshape(-1).astype(jnp.int32), value_tile.reshape(-1).astype(jnp.int32)


def tile_rows(tile):
    return pl.ds(pl.multiple_of(tile * TILE, TILE), TILE)


def score_pair(key_tile, tile_a, tile_b, keys, query_a, query_b, scores, top_rows):
    zero = jnp.zeros((TILE, HD), jnp.bfloat16)
    diagonal = jnp.concatenate(
        [
            jnp.concatenate([query_a.T, zero], axis=1),
            jnp.concatenate([zero, query_b.T], axis=1),
        ],
        axis=0,
    )
    top = None
    for begin in range(0, NW, GROUP_QK):
        parts = []
        for slot in range(begin, begin + GROUP_QK):
            key_a, key_b = key_tile[tile_a * NW + slot], key_tile[tile_b * NW + slot]
            for half in range(2):
                parts.append(
                    jnp.concatenate([keys[2 * key_a + half], keys[2 * key_b + half]], axis=1)
                )
        block = jnp.dot(
            jnp.concatenate(parts, axis=0), diagonal, preferred_element_type=jnp.float32
        )
        scores[begin * TILE : (begin + GROUP_QK) * TILE, :] = block
        partial = jnp.max(block.reshape(GROUP_QK * TILE // 8, 8, 2 * TILE), axis=0)
        top = partial if top is None else jnp.maximum(top, partial)
    top_rows[...] = top


def weigh_pair(value_tile, tile_a, tile_b, values_t, scores, top_rows):
    shift = jnp.max(top_rows[...], axis=0, keepdims=True) * TO_EXP2
    total = None
    for begin in range(0, NW, GROUP_PV):
        weights = jnp.exp2(
            scores[begin * TILE : (begin + GROUP_PV) * TILE, :] * TO_EXP2 - shift
        ).astype(jnp.bfloat16)
        picked = [
            jnp.concatenate(
                [values_t[value_tile[tile * NW + begin + i]] for i in range(GROUP_PV)], axis=1
            )
            for tile in (tile_a, tile_b)
        ]
        part = jnp.dot(
            jnp.concatenate(picked, axis=0), weights, preferred_element_type=jnp.float32
        )
        total = part if total is None else total + part
    high = HD + ONES
    out_a = total[:HD, :TILE] * (1.0 / total[HD : HD + 1, :TILE])
    out_b = total[high : high + HD, TILE:] * (1.0 / total[high + HD : high + HD + 1, TILE:])
    return out_a.T.astype(jnp.bfloat16), out_b.T.astype(jnp.bfloat16)


def partners():
    return [(dy, dx, dc) for dy in range(4) for dx in range(2) for dc in range(2)][1:]


def normalize(raw, gain, out):
    heads = raw.shape[1] // HD

    @pl.loop(0, raw.shape[0] // 16)
    def _(block):
        rows = pl.ds(pl.multiple_of(block * 16, 16), 16)
        squares = jnp.zeros((16, HD), jnp.float32)
        for head in range(heads):
            wide = raw[rows, head * HD : (head + 1) * HD].astype(jnp.float32)
            squares += wide * wide
        energy = jnp.sum(squares, axis=1, keepdims=True) * (1.0 / raw.shape[1])
        scale = lax.rsqrt(energy + EPS)
        for head in range(heads):
            columns = slice(head * HD, (head + 1) * HD)
            wide = raw[rows, columns].astype(jnp.float32)
            value = (wide * scale * gain[:, columns]).astype(jnp.bfloat16)
            if len(out.shape) == 3:
                out[head, rows, :] = value
            else:
                part = pl.ds(pl.multiple_of(block % 4 * 16, 16), 16)
                out[head, block // 4, part, :] = value


def block_kernel(
    key_tile, value_tile, query_gain, key_gain, query_rows, key_rows, value_rows, out,
    raw, query_norm, key_norm,
    queries_0, queries_1, keys_0, keys_1, values_0, values_1, turned_0, turned_1,
    attended_0, attended_1, scores_a, scores_b, top_a, top_b,
    load_sems, send_sems, recv_sems, own_sems, rim_send, rim_recv, back_send, back_recv,
):
    part, slab, place = (lax.axis_index(axis) for axis in ("dp", "blk", "uly"))
    slabs = lax.axis_size("blk")
    chip, core = place // 2, place % 2
    rows = query_rows.shape[0]
    tokens = queries_0.shape[0]
    tiles = tokens // TILE
    rim = PLANE * TILE
    queries, keys = (queries_0, queries_1), (keys_0, keys_1)
    values, turned = (values_0, values_1), (turned_0, turned_1)
    attended = (attended_0, attended_1)

    def partner(offset):
        along_y = lax.rem(chip // 2 + offset[0], 4)
        along_x = lax.rem(chip + offset[1], 2)
        return (along_y * 2 + along_x) * 2 + lax.rem(core + offset[2], 2)

    offsets = partners()
    above, below = lax.rem(slab + 1, slabs), lax.rem(slab + slabs - 1, slabs)

    loads = [
        pltpu.make_async_copy(source, raw.at[i], load_sems.at[i])
        for i, source in enumerate((key_rows, query_rows))
    ]
    for load in loads:
        load.start()

    barrier = pltpu.get_barrier_semaphore()
    for offset in offsets:
        pl.semaphore_signal(
            barrier, inc=1, device_id=(part, slab, partner(offset)), device_id_type=MESH
        )
    for other in (above, below):
        pl.semaphore_signal(barrier, inc=1, device_id=(part, other, place), device_id_type=MESH)
    pl.semaphore_wait(barrier, len(offsets) + 2)

    own_rows = pl.ds(pl.multiple_of(place * rows, 64), rows)
    own_ext = pl.ds(pl.multiple_of(rim + place * rows, 64), rows)

    def strip(kind, head, device):
        index = device * 2 + head
        if kind == 0:
            return value_rows.at[:, pl.ds(pl.multiple_of(index * HD, HD), HD)]
        return (key_norm if kind == 1 else query_norm).at[index]

    def landing(kind, head):
        if kind == 2:
            return queries[head].at[own_rows]
        if kind == 1:
            return keys[head].at[pl.ds(2 * PLANE + place * (rows // HALF), rows // HALF)]
        return values[head].at[own_ext]

    def spread(kind, head):
        phase = head * 3 + kind
        copies = []
        for i, offset in enumerate(offsets):
            device = partner(offset)
            copies.append(
                pltpu.make_async_remote_copy(
                    src_ref=strip(kind, head, device),
                    dst_ref=landing(kind, head),
                    send_sem=send_sems.at[phase, i],
                    recv_sem=recv_sems.at[phase, i],
                    device_id=(part, slab, device),
                    device_id_type=MESH,
                )
            )
        own = pltpu.make_async_copy(
            strip(kind, head, place), landing(kind, head), own_sems.at[phase]
        )
        for copy in copies:
            copy.start()
        own.start()
        return copies, own

    def arrived(group):
        for copy in group[0]:
            copy.wait_recv()
        group[1].wait()

    def pass_rims(kind, head):
        buffer = (values, keys)[kind][head]
        unit = (1, HALF)[kind]
        copies = []
        for way, (other, source, target) in enumerate(
            ((above, tokens, 0), (below, rim, rim + tokens))
        ):
            copies.append(
                pltpu.make_async_remote_copy(
                    src_ref=buffer.at[pl.ds(source // unit, rim // unit)],
                    dst_ref=buffer.at[pl.ds(target // unit, rim // unit)],
                    send_sem=rim_send.at[head * 2 + kind, way],
                    recv_sem=rim_recv.at[head * 2 + kind, way],
                    device_id=(part, other, place),
                    device_id_type=MESH,
                )
            )
        for copy in copies:
            copy.start()
        return copies

    ones = jnp.ones((ONES, TILE), jnp.bfloat16)

    def turn(head, begin, count):
        def one(step, carry):
            tile = begin + step
            turned[head][tile, :HD, :] = values[head][tile_rows(tile), :].T
            turned[head][tile, HD:, :] = ones
            return carry

        lax.fori_loop(0, count, one, 0, unroll=4)

    def back(head, step, side):
        device = lax.rem(chip + 1 + step, 8) * 2 + lax.rem(core + side, 2)
        source = attended[head].at[pl.ds(pl.multiple_of(device * rows, 64), rows)]
        column = pl.multiple_of((place * 2 + head) * HD, HD)
        return device, source, out.at[:, pl.ds(column, HD)]

    def remote_back(head, step, side):
        device, source, target = back(head, step, side)
        return pltpu.make_async_remote_copy(
            src_ref=source,
            dst_ref=target,
            send_sem=back_send.at[head, step * 2 + side],
            recv_sem=back_recv.at[head, step * 2 + side],
            device_id=(part, slab, device),
            device_id_type=MESH,
        )

    def own_back(head):
        _, source, target = back(head, 7, 0)
        return pltpu.make_async_copy(source, target, own_sems.at[6 + head])

    def attend(head):
        first = 5 * (chip + 1)

        def tile_at(position):
            return lax.rem(position + first, tiles)

        def query(tile):
            return queries[head][tile_rows(tile), :]

        def prepare(position, scores, top):
            a, b = tile_at(position), tile_at(position + 1)
            score_pair(key_tile, a, b, keys[head], query(a), query(b), scores, top)

        def finish(position, scores, top):
            a, b = tile_at(position), tile_at(position + 1)
            block = weigh_pair(value_tile, a, b, turned[head], scores, top)
            attended[head][tile_rows(a), :] = block[0]
            attended[head][tile_rows(b), :] = block[1]

        def step(i):
            position = 4 * i
            prepare(position + 2, scores_b, top_b)
            finish(position, scores_a, top_a)
            prepare(position + 4, scores_a, top_a)
            finish(position + 2, scores_b, top_b)

        prepare(0, scores_a, top_a)

        @pl.loop(0, tiles // 4)
        def _(i):
            step(i)
            phase = lax.rem(i, 5)

            @pl.when((phase != 0) & (i != 9))
            def _():
                done = lax.div(i, 5) * 4 + phase - 1
                remote_back(head, done, 0).start()
                remote_back(head, done, 1).start()

        remote_back(head, 7, 1).start()
        own_back(head).start()

    groups = {}
    rims = {}
    groups[0, 0] = spread(0, 0)
    loads[0].wait()
    normalize(raw.at[0], key_gain, key_norm)
    groups[1, 0] = spread(1, 0)
    loads[1].wait()
    normalize(raw.at[1], query_gain, query_norm)
    for head in range(2):
        turned[head][tiles + 2 * PLANE] = jnp.zeros((HD + ONES, TILE), jnp.bfloat16)
    arrived(groups[0, 0])
    groups[2, 0] = spread(2, 0)
    rims[0, 0] = pass_rims(0, 0)
    turn(0, PLANE, tiles)
    arrived(groups[1, 0])
    rims[1, 0] = pass_rims(1, 0)
    groups[0, 1] = spread(0, 1)
    for copy in rims[0, 0]:
        copy.wait()
    turn(0, 0, PLANE)
    turn(0, PLANE + tiles, PLANE)
    arrived(groups[2, 0])
    groups[1, 1] = spread(1, 1)
    groups[2, 1] = spread(2, 1)
    for copy in rims[1, 0]:
        copy.wait()
    attend(0)
    arrived(groups[0, 1])
    rims[0, 1] = pass_rims(0, 1)
    turn(1, PLANE, tiles)
    arrived(groups[1, 1])
    rims[1, 1] = pass_rims(1, 1)
    for copy in rims[0, 1]:
        copy.wait()
    turn(1, 0, PLANE)
    turn(1, PLANE + tiles, PLANE)
    arrived(groups[2, 1])
    for copy in rims[1, 1]:
        copy.wait()
    attend(1)
    for group in groups.values():
        for copy in group[0]:
            copy.wait_send()
    for head in range(2):
        for step in range(8):
            for side in range(2):
                if (step, side) != (7, 0):
                    remote_back(head, step, side).wait()
        own_back(head).wait()


def per_device(query_rows, key_rows, value_rows, query_gain, key_gain, time_start, space_start):
    rows, width = query_rows.shape
    tokens = rows * lax.axis_size("uly")
    heads = width // HD
    tiles = tokens // TILE
    extended = tokens + 2 * PLANE * TILE
    key_tile, value_tile = window_tables(time_start, space_start, tiles)
    half, full = jnp.bfloat16, jnp.float32
    anywhere = pl.BlockSpec(memory_space=pl.ANY)
    on_chip = pl.BlockSpec(memory_space=pltpu.VMEM)
    scalars = pl.BlockSpec(memory_space=pltpu.SMEM)
    count = len(partners())
    return pl.pallas_call(
        block_kernel,
        out_shape=jax.ShapeDtypeStruct((rows, width), half),
        in_specs=[scalars] * 2 + [on_chip] * 2 + [anywhere] * 3,
        out_specs=anywhere,
        scratch_shapes=[
            pltpu.VMEM((2, rows, width), half),
            pltpu.VMEM((heads, rows, HD), half),
            pltpu.VMEM((heads, rows // HALF, HALF, HD), half),
            pltpu.VMEM((tokens, HD), half),
            pltpu.VMEM((tokens, HD), half),
            pltpu.VMEM((extended // HALF, HALF, HD), half),
            pltpu.VMEM((extended // HALF, HALF, HD), half),
            pltpu.VMEM((extended, HD), half),
            pltpu.VMEM((extended, HD), half),
            pltpu.VMEM((extended // TILE + 1, HD + ONES, TILE), half),
            pltpu.VMEM((extended // TILE + 1, HD + ONES, TILE), half),
            pltpu.VMEM((tokens, HD), half),
            pltpu.VMEM((tokens, HD), half),
            pltpu.VMEM((NW * TILE, 2 * TILE), full),
            pltpu.VMEM((NW * TILE, 2 * TILE), full),
            pltpu.VMEM((8, 2 * TILE), full),
            pltpu.VMEM((8, 2 * TILE), full),
            pltpu.SemaphoreType.DMA((2,)),
            pltpu.SemaphoreType.DMA((6, count)),
            pltpu.SemaphoreType.DMA((6, count)),
            pltpu.SemaphoreType.DMA((8,)),
            pltpu.SemaphoreType.DMA((4, 2)),
            pltpu.SemaphoreType.DMA((4, 2)),
            pltpu.SemaphoreType.DMA((2, 16)),
            pltpu.SemaphoreType.DMA((2, 16)),
        ],
        compiler_params=pltpu.CompilerParams(
            collective_id=0, has_side_effects=True, vmem_limit_bytes=56 * 2**20
        ),
        cost_estimate=pl.CostEstimate(
            flops=8 * tokens * NW * TILE * HD,
            bytes_accessed=8 * rows * width,
            transcendentals=2 * tokens * NW * TILE,
        ),
    )(
        key_tile, value_tile, query_gain.reshape(1, width), key_gain.reshape(1, width),
        query_rows, key_rows, value_rows,
    )


def solution(mesh):
    rows = P(("dp", "blk", "uly"), None)
    return jax.shard_map(
        per_device,
        mesh=mesh,
        in_specs=(rows, rows, rows, P(), P(), P(), P()),
        out_specs=rows,
        check_vma=False,
    )
```

time: 246 us -> 142 us (0.58)
  waiting for transfers between devices: 109 us -> 0 us
  Pallas kernels: 46.8 us -> 134 us
  blocking collectives: 39 us -> 0 us
  starting transfers between devices: 28.8 us -> 0 us
  local copies, waits for them, and re-layouts: 16.1 us -> 5.67 us
  other arithmetic: 5.75 us -> 0.87 us
    pallas_call x1, Pallas kernels: 46.8 us -> 134 us  [per_device(): pl.pallas_call(block_kernel, out_shape=jax.ShapeDtypeStruct((rows, width)...]
    all_to_all x3 -> x0, waiting for transfers between devices: 74.4 us -> none  [to_heads(): return lax.all_to_all(rows, 'uly', split_axis=1, concat_axis=0, tiled=True)]
    all_to_all x1 -> x0, blocking collectives: 39 us -> none  [per_device(): lax.all_to_all(attended, 'uly', split_axis=0, concat_axis=1, tiled=True)]
    ppermute x4 -> x0, waiting for transfers between devices: 34.6 us -> none  [the longest x2 26.5 us: halo(): below = lax.ppermute(rows[rows.shape[0] - rim:], 'blk', up)]
    all_to_all x3 -> x0, starting transfers between devices: 17.3 us -> none  [to_heads(): return lax.all_to_all(rows, 'uly', split_axis=1, concat_axis=0, tiled=True)]
    ppermute x4 -> x0, starting transfers between devices: 11.4 us -> none  [the longest x2 8.85 us: halo(): below = lax.ppermute(rows[rows.shape[0] - rim:], 'blk', up)]
    all_to_all x4 -> x0, local copies, waits for them, and re-layouts: 8.8 us -> none  [the longest x3 6.98 us: to_heads(): return lax.all_to_all(rows, 'uly', split_axis=1, concat_axis=0, tiled=True)]
    slice x2 -> x0, local copies, waits for them, and re-layouts: 5.31 us -> none  [halo(): above = lax.ppermute(rows[:rim], 'blk', down)]
  transfers between devices with their start and end apart: 7 -> 0, of which waited for: 7 -> 0; matrix products, arithmetic and copies ran while one was open for 5% -> 0% of each run, Pallas kernels for 0% -> 0%
where the time goes in v2:
time: 142 us; the launch traced here: 141 us
  Pallas kernels  134 us (94%)
  local copies, waits for them, and re-layouts  5.67 us (4%)
    pallas_call x1, Pallas kernels, per_device(): pl.pallas_call(block_kernel, out_shape=jax.ShapeDtypeStruct((rows, width)...  134 us
    unnamed x3, local copies, waits for them, and re-layouts  4.19 us

profile of v2, /device:TPU:1, one launch (start us, length us, event | category | flops | bytes accessed | tf_op | source)
XLA Modules:
  0.0 140.7 jit_solution(8858500472372754938)
XLA Ops:
  0.0 0.0 copy-start
  0.0 0.7 copy-done
  0.7 0.1 constant_dynamic-slice_fusion
  0.8 0.8 bitcast_add_fusion
  1.5 0.1 fusion.9
  1.6 0.7 reshape.161.value_tile
  2.3 0.7 reshape.159.key_tile
  3.0 134.2 %shard_map.73 = bf16[320,4096]{1,0:T(8,128)(2,1)} custom-call(s32[720]{0:T(1024)} %reshape.159.key_tile, s32[720]{0:T(1024)} %reshape.161.value_tile, f32[1,4096]{1,0:T(1,128)} %bitcast.6, f32[1,4096]{1,0:T(1,128)} %bitcast.7, bf16[320,4096]{1,0:T(8,128)(2,1)} %query_rows.1, bf16[320,4096]{1,0:T(8,128)(2,1)} %key_rows.1, bf16[320,4096]{1,0:T(8,128)(2,1)} %value_rows.1), custom_call_target="tpu_custom_call" | custom-call | flops 12079595520 | bytes 10485760 | tf_op jit(solution)/shard_map/pallas_call | solution.py:377
  137.2 3.5 %copy.9 = bf16[320,4096]{1,0:T(8,128)(2,1)} copy(bf16[320,4096]{1,0:T(8,128)(2,1)} %shard_map.73) | data formatting | bytes 5242880
  (3 shorter events, 0.0 us)
Async XLA Ops:
  0.0 0.7 copy-start

commit v3 on v2

--- a/solution.py
+++ b/solution.py
@@ -24,6 +24,8 @@
 ONES = 16
 GROUP_QK = 6
 GROUP_PV = 9
+SENT = 10
+MIDWAY = 4
 
 
 def window_tables(time_start, space_start, slab_tiles):
@@ -104,7 +106,8 @@
 
 
 def partners():
-    return [(dy, dx, dc) for dy in range(4) for dx in range(2) for dc in range(2)][1:]
+    order = [(dy, dx, dc) for dc in range(2) for dx in (1, 0) for dy in (2, 1, 3, 0)]
+    return [offset for offset in order if any(offset)]
 
 
 def normalize(raw, gain, out):
@@ -188,7 +191,7 @@
             return keys[head].at[pl.ds(2 * PLANE + place * (rows // HALF), rows // HALF)]
         return values[head].at[own_ext]
 
-    def spread(kind, head):
+    def remote(kind, head):
         phase = head * 3 + kind
         copies = []
         for i, offset in enumerate(offsets):
@@ -203,20 +206,24 @@
                     device_id_type=MESH,
                 )
             )
-        own = pltpu.make_async_copy(
-            strip(kind, head, place), landing(kind, head), own_sems.at[phase]
+        return copies
+
+    def local(kind, head):
+        return pltpu.make_async_copy(
+            strip(kind, head, place), landing(kind, head), own_sems.at[head * 3 + kind]
         )
-        for copy in copies:
+
+    def spread(kind, head):
+        for copy in remote(kind, head):
             copy.start()
-        own.start()
-        return copies, own
-
-    def arrived(group):
-        for copy in group[0]:
+        local(kind, head).start()
+
+    def arrived(kind, head):
+        for copy in remote(kind, head):
             copy.wait_recv()
-        group[1].wait()
-
-    def pass_rims(kind, head):
+        local(kind, head).wait()
+
+    def rims(kind, head):
         buffer = (values, keys)[kind][head]
         unit = (1, HALF)[kind]
         copies = []
@@ -233,9 +240,15 @@
                     device_id_type=MESH,
                 )
             )
-        for copy in copies:
+        return copies
+
+    def pass_rims(kind, head):
+        for copy in rims(kind, head):
             copy.start()
-        return copies
+
+    def rims_arrived(kind, head):
+        for copy in rims(kind, head):
+            copy.wait()
 
     ones = jnp.ones((ONES, TILE), jnp.bfloat16)
 
@@ -269,7 +282,7 @@
         _, source, target = back(head, 7, 0)
         return pltpu.make_async_copy(source, target, own_sems.at[6 + head])
 
-    def attend(head):
+    def attend(head, midway=None):
         first = 5 * (chip + 1)
 
         def tile_at(position):
@@ -301,59 +314,70 @@
         def _(i):
             step(i)
             phase = lax.rem(i, 5)
-
-            @pl.when((phase != 0) & (i != 9))
-            def _():
-                done = lax.div(i, 5) * 4 + phase - 1
-                remote_back(head, done, 0).start()
-                remote_back(head, done, 1).start()
-
-        remote_back(head, 7, 1).start()
-        own_back(head).start()
-
-    groups = {}
-    rims = {}
-    groups[0, 0] = spread(0, 0)
+            if midway is not None:
+                pl.when(i == MIDWAY)(midway)
+            if head == 1:
+
+                @pl.when((phase != 0) & (i != 9))
+                def _():
+                    done = lax.div(i, 5) * 4 + phase - 1
+                    remote_back(head, done, 0).start()
+                    remote_back(head, done, 1).start()
+
+        if head == 1:
+            remote_back(head, 7, 1).start()
+            own_back(head).start()
+
+    spread(0, 0)
     loads[0].wait()
     normalize(raw.at[0], key_gain, key_norm)
-    groups[1, 0] = spread(1, 0)
+    spread(1, 0)
     loads[1].wait()
     normalize(raw.at[1], query_gain, query_norm)
     for head in range(2):
         turned[head][tiles + 2 * PLANE] = jnp.zeros((HD + ONES, TILE), jnp.bfloat16)
-    arrived(groups[0, 0])
-    groups[2, 0] = spread(2, 0)
-    rims[0, 0] = pass_rims(0, 0)
+    arrived(0, 0)
+    spread(2, 0)
+    pass_rims(0, 0)
     turn(0, PLANE, tiles)
-    arrived(groups[1, 0])
-    rims[1, 0] = pass_rims(1, 0)
-    groups[0, 1] = spread(0, 1)
-    for copy in rims[0, 0]:
-        copy.wait()
+    arrived(1, 0)
+    pass_rims(1, 0)
+    spread(0, 1)
+    rims_arrived(0, 0)
     turn(0, 0, PLANE)
     turn(0, PLANE + tiles, PLANE)
-    arrived(groups[2, 0])
-    groups[1, 1] = spread(1, 1)
-    groups[2, 1] = spread(2, 1)
-    for copy in rims[1, 0]:
-        copy.wait()
-    attend(0)
-    arrived(groups[0, 1])
-    rims[0, 1] = pass_rims(0, 1)
-    turn(1, PLANE, tiles)
-    arrived(groups[1, 1])
-    rims[1, 1] = pass_rims(1, 1)
-    for copy in rims[0, 1]:
-        copy.wait()
+    arrived(2, 0)
+    spread(1, 1)
+    spread(2, 1)
+    rims_arrived(1, 0)
+
+    def values_on():
+        arrived(0, 1)
+        pass_rims(0, 1)
+        turn(1, PLANE, tiles)
+
+    attend(0, values_on)
+    arrived(1, 1)
+    pass_rims(1, 1)
+    rims_arrived(0, 1)
     turn(1, 0, PLANE)
     turn(1, PLANE + tiles, PLANE)
-    arrived(groups[2, 1])
-    for copy in rims[1, 1]:
-        copy.wait()
+    leaving = remote(2, 1)
+    for copy in leaving[:SENT]:
+        copy.wait_send()
+    for done in range(7):
+        remote_back(0, done, 0).start()
+        remote_back(0, done, 1).start()
+    remote_back(0, 7, 1).start()
+    own_back(0).start()
+    arrived(2, 1)
+    rims_arrived(1, 1)
     attend(1)
-    for group in groups.values():
-        for copy in group[0]:
+    for kind, head in ((0, 0), (1, 0), (2, 0), (0, 1), (1, 1)):
+        for copy in remote(kind, head):
             copy.wait_send()
+    for copy in leaving[SENT:]:
+        copy.wait_send()
     for head in range(2):
         for step in range(8):
             for side in range(2):
@@ -376,7 +400,7 @@
     count = len(partners())
     return pl.pallas_call(
         block_kernel,
-        out_shape=jax.ShapeDtypeStruct((rows, width), half),
+        out_shape=pltpu.VMEM((rows, width), half),
         in_specs=[scalars] * 2 + [on_chip] * 2 + [anywhere] * 3,
         out_specs=anywhere,
         scratch_shapes=[

time: 142 us -> 131 us (0.923)
  Pallas kernels: 134 us -> 126 us
  local copies, waits for them, and re-layouts: 5.67 us -> 3.63 us
    pallas_call x1, Pallas kernels: 134 us -> 126 us  [per_device(): pl.pallas_call(block_kernel, out_shape=pltpu.VMEM((rows, width), half), i...]
    unnamed x3, local copies, waits for them, and re-layouts: 4.19 us -> 2.16 us
where the time goes in v3:
time: 131 us
  Pallas kernels  126 us (96%)
  local copies, waits for them, and re-layouts  3.63 us (3%)
    pallas_call x1, Pallas kernels, per_device(): pl.pallas_call(block_kernel, out_shape=pltpu.VMEM((rows, width), half), i...  126 us

profile of v3, /device:TPU:1, one launch (start us, length us, event | category | flops | bytes accessed | tf_op | source)
XLA Modules:
  0.0 130.7 jit_solution(11705207154145555471)
XLA Ops:
  0.0 0.0 copy-start
  0.0 0.7 copy-done
  0.7 0.1 constant_dynamic-slice_fusion
  0.8 0.8 bitcast_add_fusion
  1.5 0.1 fusion.9
  1.6 0.7 reshape.161.value_tile
  2.3 0.7 reshape.159.key_tile
  3.0 126.2 %shard_map.73 = bf16[320,4096]{1,0:T(8,128)(2,1)S(1)} custom-call(s32[720]{0:T(1024)} %reshape.159.key_tile, s32[720]{0:T(1024)} %reshape.161.value_tile, f32[1,4096]{1,0:T(1,128)} %bitcast.6, f32[1,4096]{1,0:T(1,128)} %bitcast.7, bf16[320,4096]{1,0:T(8,128)(2,1)} %query_rows.1, bf16[320,4096]{1,0:T(8,128)(2,1)} %key_rows.1, bf16[320,4096]{1,0:T(8,128)(2,1)} %value_rows.1), custom_call_target="tpu_custom_call" | custom-call | flops 12079595520 | bytes 10485760 | tf_op jit(solution)/shard_map/pallas_call | solution.py:401
  129.2 1.5 %copy.9 = bf16[320,4096]{1,0:T(8,128)(2,1)} copy(bf16[320,4096]{1,0:T(8,128)(2,1)S(1)} %shard_map.73) | data formatting | bytes 5242880
  (3 shorter events, 0.0 us)
Async XLA Ops:
  0.0 0.7 copy-start

commit v4 on v3

--- a/solution.py
+++ b/solution.py
@@ -28,27 +28,29 @@
 MIDWAY = 4
 
 
-def window_tables(time_start, space_start, slab_tiles):
-    first = lax.axis_index("blk") * slab_tiles
-    grid_time = slab_tiles // PLANE * lax.axis_size("blk")
-    starts_time = lax.dynamic_slice_in_dim(time_start, first, slab_tiles)
-    starts_space = lax.dynamic_slice_in_dim(space_start, first, slab_tiles, 1)
-    local = jnp.arange(slab_tiles, dtype=jnp.int32)
-    tile_ids = first + local
-    slot = jnp.arange(NW, dtype=jnp.int32)[None, :]
-    span_time = (tile_ids // PLANE + starts_time)[:, None] + slot // (WIN_H * WIN_W)
-    span_height = (tile_ids % PLANE // TILES_W + starts_space[0])[:, None] + slot // WIN_W % WIN_H
-    span_width = (tile_ids % TILES_W + starts_space[1])[:, None] + slot % WIN_W
-    valid = (span_time >= 0) & (span_time < grid_time)
-    valid = valid & (span_height >= 0) & (span_height < TILES_H)
-    valid = valid & (span_width >= 0) & (span_width < TILES_W)
-    local_time = span_time - first // PLANE + 1
-    index = (local_time * TILES_H + span_height) * TILES_W + span_width
-    own = (local + PLANE)[:, None]
-    zero_tile = slab_tiles + 2 * PLANE
-    key_tile = jnp.where(valid, index, own)
-    value_tile = jnp.where(valid, index, zero_tile)
-    return key_tile.reshape(-1).astype(jnp.int32), value_tile.reshape(-1).astype(jnp.int32)
+def window_tables(time_start, space_start, key_tile, value_tile, slab, slabs, tiles):
+    slab_times = tiles // PLANE
+
+    @pl.loop(0, tiles)
+    def _(tile):
+        number = slab * tiles + tile
+        time = lax.div(tile, PLANE) + 1 + time_start[number]
+        height = lax.rem(lax.div(tile, TILES_W), TILES_H) + space_start[0, number]
+        width = lax.rem(tile, TILES_W) + space_start[1, number]
+        lowest = 1 - slab * slab_times
+        widths = [(width + k, (width + k >= 0) & (width + k < TILES_W)) for k in range(WIN_W)]
+        for i in range(WIN_T):
+            at_time = time + i
+            in_time = (at_time >= lowest) & (at_time < lowest + slab_times * slabs)
+            for j in range(WIN_H):
+                at_height = height + j
+                inside = in_time & (at_height >= 0) & (at_height < TILES_H)
+                base = at_time * PLANE + at_height * TILES_W
+                for k, (at_width, in_width) in enumerate(widths):
+                    valid = inside & in_width
+                    slot = tile * NW + (i * WIN_H + j) * WIN_W + k
+                    key_tile[slot] = jnp.where(valid, base + at_width, tile + PLANE)
+                    value_tile[slot] = jnp.where(valid, base + at_width, tiles + 2 * PLANE)
 
 
 def tile_rows(tile):
@@ -134,10 +136,11 @@
 
 
 def block_kernel(
-    key_tile, value_tile, query_gain, key_gain, query_rows, key_rows, value_rows, out,
+    time_start, space_start, query_gain, key_gain, query_rows, key_rows, value_rows, out,
     raw, query_norm, key_norm,
     queries_0, queries_1, keys_0, keys_1, values_0, values_1, turned_0, turned_1,
     attended_0, attended_1, scores_a, scores_b, top_a, top_b,
+    key_tile, value_tile,
     load_sems, send_sems, recv_sems, own_sems, rim_send, rim_recv, back_send, back_recv,
 ):
     part, slab, place = (lax.axis_index(axis) for axis in ("dp", "blk", "uly"))
@@ -334,6 +337,7 @@
     spread(1, 0)
     loads[1].wait()
     normalize(raw.at[1], query_gain, query_norm)
+    window_tables(time_start, space_start, key_tile, value_tile, slab, slabs, tiles)
     for head in range(2):
         turned[head][tiles + 2 * PLANE] = jnp.zeros((HD + ONES, TILE), jnp.bfloat16)
     arrived(0, 0)
@@ -392,7 +396,6 @@
     heads = width // HD
     tiles = tokens // TILE
     extended = tokens + 2 * PLANE * TILE
-    key_tile, value_tile = window_tables(time_start, space_start, tiles)
     half, full = jnp.bfloat16, jnp.float32
     anywhere = pl.BlockSpec(memory_space=pl.ANY)
     on_chip = pl.BlockSpec(memory_space=pltpu.VMEM)
@@ -421,6 +424,8 @@
             pltpu.VMEM((NW * TILE, 2 * TILE), full),
             pltpu.VMEM((8, 2 * TILE), full),
             pltpu.VMEM((8, 2 * TILE), full),
+            pltpu.SMEM((tiles * NW,), jnp.int32),
+            pltpu.SMEM((tiles * NW,), jnp.int32),
             pltpu.SemaphoreType.DMA((2,)),
             pltpu.SemaphoreType.DMA((6, count)),
             pltpu.SemaphoreType.DMA((6, count)),
@@ -439,7 +444,7 @@
             transcendentals=2 * tokens * NW * TILE,
         ),
     )(
-        key_tile, value_tile, query_gain.reshape(1, width), key_gain.reshape(1, width),
+        time_start, space_start, query_gain.reshape(1, width), key_gain.reshape(1, width),
         query_rows, key_rows, value_rows,
     )
 

time: 131 us -> 128 us (0.977)
  local copies, waits for them, and re-layouts: 3.63 us -> 1.49 us
    select_n x2 -> x0, local copies, waits for them, and re-layouts: 1.4 us -> none  [the longest x1 0.7 us: window_tables(): key_tile = jnp.where(valid, index, own)]
where the time goes in v4:
time: 128 us
  Pallas kernels  126 us (98%)
  local copies, waits for them, and re-layouts  1.49 us (1%)
    pallas_call x1, Pallas kernels, per_device(): pl.pallas_call(block_kernel, out_shape=pltpu.VMEM((rows, width), half), i...  126 us

profile of v4, /device:TPU:1, one launch (start us, length us, event | category | flops | bytes accessed | tf_op | source)
XLA Modules:
  0.0 127.7 jit_solution(5364909303230549463)
XLA Ops:
  0.0 126.2 %shard_map.73 = bf16[320,4096]{1,0:T(8,128)(2,1)S(1)} custom-call(s32[160]{0:T(256)} %time_start.1, s32[2,160]{1,0:T(2,128)} %space_start.1, f32[1,4096]{1,0:T(1,128)} %bitcast.2, f32[1,4096]{1,0:T(1,128)} %bitcast.3, bf16[320,4096]{1,0:T(8,128)(2,1)} %query_rows.1, bf16[320,4096]{1,0:T(8,128)(2,1)} %key_rows.1, bf16[320,4096]{1,0:T(8,128)(2,1)} %value_rows.1), custom_call_target="tpu_custom_call" | custom-call | flops 12079595520 | bytes 10485760 | tf_op jit(solution)/shard_map/pallas_call | solution.py:404
  126.2 1.5 %copy.9 = bf16[320,4096]{1,0:T(8,128)(2,1)} copy(bf16[320,4096]{1,0:T(8,128)(2,1)S(1)} %shard_map.73) | data formatting | bytes 5242880

commit v5 on v4

--- a/solution.py
+++ b/solution.py
@@ -136,11 +136,11 @@
 
 
 def block_kernel(
-    time_start, space_start, query_gain, key_gain, query_rows, key_rows, value_rows, out,
+    times_in, spaces_in, query_gain_in, key_gain_in, query_rows, key_rows, value_rows, out,
     raw, query_norm, key_norm,
     queries_0, queries_1, keys_0, keys_1, values_0, values_1, turned_0, turned_1,
     attended_0, attended_1, scores_a, scores_b, top_a, top_b,
-    key_tile, value_tile,
+    key_tile, value_tile, time_start, space_start, query_gain, key_gain,
     load_sems, send_sems, recv_sems, own_sems, rim_send, rim_recv, back_send, back_recv,
 ):
     part, slab, place = (lax.axis_index(axis) for axis in ("dp", "blk", "uly"))
@@ -163,11 +163,18 @@
     above, below = lax.rem(slab + 1, slabs), lax.rem(slab + slabs - 1, slabs)
 
     loads = [
-        pltpu.make_async_copy(source, raw.at[i], load_sems.at[i])
-        for i, source in enumerate((key_rows, query_rows))
+        pltpu.make_async_copy(source, target, load_sems.at[i])
+        for i, (source, target) in enumerate(
+            (
+                (key_rows, raw.at[0]),
+                (query_rows, raw.at[1]),
+                (key_gain_in, key_gain),
+                (query_gain_in, query_gain),
+                (times_in, time_start),
+                (spaces_in, space_start),
+            )
+        )
     ]
-    for load in loads:
-        load.start()
 
     barrier = pltpu.get_barrier_semaphore()
     for offset in offsets:
@@ -332,11 +339,17 @@
             own_back(head).start()
 
     spread(0, 0)
+    for load in loads:
+        load.start()
+    loads[2].wait()
     loads[0].wait()
     normalize(raw.at[0], key_gain, key_norm)
     spread(1, 0)
+    loads[3].wait()
     loads[1].wait()
     normalize(raw.at[1], query_gain, query_norm)
+    loads[4].wait()
+    loads[5].wait()
     window_tables(time_start, space_start, key_tile, value_tile, slab, slabs, tiles)
     for head in range(2):
         turned[head][tiles + 2 * PLANE] = jnp.zeros((HD + ONES, TILE), jnp.bfloat16)
@@ -374,12 +387,12 @@
         remote_back(0, done, 1).start()
     remote_back(0, 7, 1).start()
     own_back(0).start()
+    for kind, head in ((0, 0), (1, 0), (2, 0), (0, 1), (1, 1)):
+        for copy in remote(kind, head):
+            copy.wait_send()
     arrived(2, 1)
     rims_arrived(1, 1)
     attend(1)
-    for kind, head in ((0, 0), (1, 0), (2, 0), (0, 1), (1, 1)):
-        for copy in remote(kind, head):
-            copy.wait_send()
     for copy in leaving[SENT:]:
         copy.wait_send()
     for head in range(2):
@@ -398,13 +411,11 @@
     extended = tokens + 2 * PLANE * TILE
     half, full = jnp.bfloat16, jnp.float32
     anywhere = pl.BlockSpec(memory_space=pl.ANY)
-    on_chip = pl.BlockSpec(memory_space=pltpu.VMEM)
-    scalars = pl.BlockSpec(memory_space=pltpu.SMEM)
     count = len(partners())
     return pl.pallas_call(
         block_kernel,
         out_shape=pltpu.VMEM((rows, width), half),
-        in_specs=[scalars] * 2 + [on_chip] * 2 + [anywhere] * 3,
+        in_specs=[anywhere] * 7,
         out_specs=anywhere,
         scratch_shapes=[
             pltpu.VMEM((2, rows, width), half),
@@ -426,7 +437,11 @@
             pltpu.VMEM((8, 2 * TILE), full),
             pltpu.SMEM((tiles * NW,), jnp.int32),
             pltpu.SMEM((tiles * NW,), jnp.int32),
-            pltpu.SemaphoreType.DMA((2,)),
+            pltpu.SMEM(time_start.shape, jnp.int32),
+            pltpu.SMEM(space_start.shape, jnp.int32),
+            pltpu.VMEM((1, width), full),
+            pltpu.VMEM((1, width), full),
+            pltpu.SemaphoreType.DMA((6,)),
             pltpu.SemaphoreType.DMA((6, count)),
             pltpu.SemaphoreType.DMA((6, count)),
             pltpu.SemaphoreType.DMA((8,)),

time: 128 us -> 127 us (level)
  no operation moved by 1% of the time
where the time goes in v5:
time: 127 us
  Pallas kernels  125 us (98%)
  local copies, waits for them, and re-layouts  1.49 us (1%)
    pallas_call x1, Pallas kernels, per_device(): pl.pallas_call(block_kernel, out_shape=pltpu.VMEM((rows, width), half), i...  125 us

profile of v5, /device:TPU:1, one launch (start us, length us, event | category | flops | bytes accessed | tf_op | source)
XLA Modules:
  0.0 126.9 jit_solution(63922889432282827)
XLA Ops:
  0.0 125.4 %shard_map.73 = bf16[320,4096]{1,0:T(8,128)(2,1)S(1)} custom-call(s32[160]{0:T(256)} %times_in.1, s32[2,160]{1,0:T(2,128)} %spaces_in.1, f32[1,4096]{1,0:T(1,128)} %bitcast.2, f32[1,4096]{1,0:T(1,128)} %bitcast.3, bf16[320,4096]{1,0:T(8,128)(2,1)} %query_rows.1, bf16[320,4096]{1,0:T(8,128)(2,1)} %key_rows.1, bf16[320,4096]{1,0:T(8,128)(2,1)} %value_rows.1), custom_call_target="tpu_custom_call" | custom-call | flops 12079595520 | bytes 10485760 | tf_op jit(solution)/shard_map/pallas_call | solution.py:415
  125.4 1.5 %copy.9 = bf16[320,4096]{1,0:T(8,128)(2,1)} copy(bf16[320,4096]{1,0:T(8,128)(2,1)S(1)} %shard_map.73) | data formatting | bytes 5242880

commit v6 on v5

--- a/solution.py
+++ b/solution.py
@@ -271,8 +271,11 @@
 
         lax.fori_loop(0, count, one, 0, unroll=4)
 
+    def target_chip(step):
+        return lax.rem(chip + 9 + step + core * (6 - 2 * step), 8)
+
     def back(head, step, side):
-        device = lax.rem(chip + 1 + step, 8) * 2 + lax.rem(core + side, 2)
+        device = target_chip(step) * 2 + lax.rem(core + side, 2)
         source = attended[head].at[pl.ds(pl.multiple_of(device * rows, 64), rows)]
         column = pl.multiple_of((place * 2 + head) * HD, HD)
         return device, source, out.at[:, pl.ds(column, HD)]
@@ -293,10 +296,9 @@
         return pltpu.make_async_copy(source, target, own_sems.at[6 + head])
 
     def attend(head, midway=None):
-        first = 5 * (chip + 1)
-
         def tile_at(position):
-            return lax.rem(position + first, tiles)
+            step = lax.div(jnp.minimum(position, tiles - 1), 5)
+            return target_chip(step) * 5 + lax.rem(position, 5)
 
         def query(tile):
             return queries[head][tile_rows(tile), :]

time: 127 us -> 126 us (level)
    pallas_call x1, Pallas kernels: 125 us -> 124 us  [per_device(): pl.pallas_call(block_kernel, out_shape=pltpu.VMEM((rows, width), half), i...]
where the time goes in v6:
time: 126 us
  Pallas kernels  124 us (98%)
  local copies, waits for them, and re-layouts  1.49 us (1%)
    pallas_call x1, Pallas kernels, per_device(): pl.pallas_call(block_kernel, out_shape=pltpu.VMEM((rows, width), half), i...  124 us

profile of v6, /device:TPU:1, one launch (start us, length us, event | category | flops | bytes accessed | tf_op | source)
XLA Modules:
  0.0 125.5 jit_solution(7316716135476492354)
XLA Ops:
  0.0 124.0 %shard_map.73 = bf16[320,4096]{1,0:T(8,128)(2,1)S(1)} custom-call(s32[160]{0:T(256)} %times_in.1, s32[2,160]{1,0:T(2,128)} %spaces_in.1, f32[1,4096]{1,0:T(1,128)} %bitcast.2, f32[1,4096]{1,0:T(1,128)} %bitcast.3, bf16[320,4096]{1,0:T(8,128)(2,1)} %query_rows.1, bf16[320,4096]{1,0:T(8,128)(2,1)} %key_rows.1, bf16[320,4096]{1,0:T(8,128)(2,1)} %value_rows.1), custom_call_target="tpu_custom_call" | custom-call | flops 12079595520 | bytes 10485760 | tf_op jit(solution)/shard_map/pallas_call | solution.py:417
  124.0 1.5 %copy.9 = bf16[320,4096]{1,0:T(8,128)(2,1)} copy(bf16[320,4096]{1,0:T(8,128)(2,1)S(1)} %shard_map.73) | data formatting | bytes 5242880
